TPU v7x, 32 devices: a whole 2x2x4 slice. The times are simulated.
32 devices in a mesh: groups: 2 (over x), gy: 16 (over z, y, core).
Axes of the slice: x: 2, y: 2, z: 4, core: 2. Of those that a mesh axis runs over, the one named last changes fastest.
Arguments:
- tiles: bfloat16 [1024, 16, 128], P(('groups', 'gy')), parts along dimension 0, may hold values from -6 to 6
- entry_dest: int32 [1024, 1], P('groups'), parts along dimension 0, may hold values from 0 to 15; in each aligned block of 32 rows (0 to 31, 32 to 63, ...) at most 4 rows name the same one
- entry_tile: int32 [1024], P('groups'), parts along dimension 0, may hold values from 0 to 31
- entry_z: int32 [1024], P('groups'), parts along dimension 0, may hold values from 0 to 3
- entry_xb: int32 [1024], P('groups'), parts along dimension 0, may hold values from 0 to 3
- entry_ky: int32 [1024], P('groups'), parts along dimension 0, may hold values from 0 to 7
- entry_kx: int32 [1024], P('groups'), parts along dimension 0, may hold values from 0 to 7
- wy_table: bfloat16 [8, 8, 16], replicated, may hold values from 0 to 1
- wx_table: bfloat16 [8, 128, 128], replicated, may hold values from 0 to 1
- w_first: bfloat16 [32, 1, 3, 3, 3], replicated, may hold values from -1.25 to 1.25
- b_first: float32 [32], replicated, may hold values from -1.5 to 1.5
- w_second: bfloat16 [32, 32, 3, 3, 3], replicated, may hold values from -0.21875 to 0.21875
- b_second: float32 [32], replicated, may hold values from -1.5 to 1.5
- w_third: bfloat16 [32, 32, 3, 3, 3], replicated, may hold values from -0.21875 to 0.21875
- b_third: float32 [32], replicated, may hold values from -1.5 to 1.5
Outputs:
- affinity_features: bfloat16 [32, 8, 128, 512], P(None, 'groups', 'gy'), parts along dimension 1
There are 2 independent parts, one for each index of `groups`. A program takes and returns all parts, laid end to end along the dimension named above; an argument that names none is the same for every part. Nothing has to cross between parts.
Inputs may be any that keep to these rules, and one draw needn't show every extreme that they name: `entry_dest`: rows 32 * s to 32 * s + 31 are the entries of the tiles of device s of gy; among one device's rows no brick is named more than 4 times, a bound that some block reaches.
All inputs are finite; a program needn't handle non-finite values.
Results may differ from a plain program's by a relative error of at most 0.0064.
Values may be sent and summed in bfloat16 or wider, within the bound.
No kernel may reach another device: no remote copies, remote signals or barrier semaphores. Data moves between devices by JAX's collectives and lax.ppermute only.
A program may use at most 64 MiB of HBM per device.

v0:
```python
import jax
import jax.numpy as jnp
from jax import lax
from jax.sharding import PartitionSpec as P

X = 512
YB = 8
Z = 4
CAP = 4


def with_halo(cells, sides, width):
    for axis, dim in sides:
        count = lax.axis_size(axis)
        ends = count - 1
        head = lax.slice_in_dim(cells, 0, width, axis=dim)
        tail = lax.slice_in_dim(cells, cells.shape[dim] - width, cells.shape[dim], axis=dim)
        cells = jnp.concatenate(
            [
                lax.ppermute(tail, axis, [(i, (i + 1) % count) for i in range(ends)]),
                cells,
                lax.ppermute(head, axis, [((i + 1) % count, i) for i in range(ends)]),
            ],
            axis=dim,
        )
    return cells


def convolve(padded, weight, bias):
    result = lax.conv_general_dilated(
        padded[None],
        weight,
        (1, 1, 1),
        ((1, 1), (0, 0), (1, 1)),
        dimension_numbers=("NCDHW", "OIDHW", "NCDHW"),
        preferred_element_type=jnp.float32,
    )[0]
    return jax.nn.relu(result + bias[:, None, None, None])


def on_device(
    tiles,
    entry_dest,
    entry_tile,
    entry_z,
    entry_xb,
    entry_ky,
    entry_kx,
    wy_table,
    wx_table,
    w_first,
    b_first,
    w_second,
    b_second,
    w_third,
    b_third,
):
    devices_gy = lax.axis_size("gy")
    own_index = lax.axis_index("gy")
    tiles_dev, tile_rows, tile_cols = tiles.shape
    per_device = entry_dest.shape[0] // devices_gy
    slot_total = devices_gy * CAP
    target_brick = entry_dest[:, 0].reshape(devices_gy, per_device)
    later_pos = lax.broadcasted_iota(jnp.int32, (per_device, per_device), 0)
    earlier_pos = lax.broadcasted_iota(jnp.int32, (per_device, per_device), 1)
    same_brick = (target_brick[:, :, None] == target_brick[:, None, :]) & (earlier_pos < later_pos)[
        None
    ]
    slot_rank = jnp.sum(same_brick, axis=2, dtype=jnp.int32)
    capacity_iota = lax.broadcasted_iota(jnp.int32, (1, CAP, 1), 1)
    matched = (
        (target_brick == own_index)[:, None, :] & (slot_rank[:, None, :] == capacity_iota)
    ).astype(jnp.float32)
    slot_live = jnp.sum(matched, axis=2).reshape(-1) > 0.5

    def slot_field(field):
        return (
            jnp.sum(matched * field.reshape(devices_gy, 1, per_device).astype(jnp.float32), axis=2)
            .reshape(-1)
            .astype(jnp.int32)
        )

    slot_z = slot_field(entry_z)
    slot_xb = slot_field(entry_xb)
    slot_ky = slot_field(entry_ky)
    slot_kx = slot_field(entry_kx)
    local_tiles = tiles.reshape(tiles_dev, tile_rows * tile_cols)
    own_brick = lax.dynamic_index_in_dim(target_brick, own_index, 0, keepdims=False)
    own_rank = lax.dynamic_index_in_dim(slot_rank, own_index, 0, keepdims=False)
    own_tile = lax.dynamic_index_in_dim(
        entry_tile.reshape(devices_gy, per_device), own_index, 0, keepdims=False
    )
    slot_target = own_brick * CAP + own_rank
    chooser = (
        lax.broadcasted_iota(jnp.int32, (slot_total, per_device), 0) == slot_target[None, :]
    ).astype(jnp.bfloat16)
    tile_choice = (
        own_tile[:, None] == lax.broadcasted_iota(jnp.int32, (per_device, tiles_dev), 1)
    ).astype(jnp.bfloat16)
    pick_matrix = jnp.dot(chooser, tile_choice, preferred_element_type=jnp.float32).astype(
        jnp.bfloat16
    )
    send_buffer = jnp.dot(pick_matrix, local_tiles, preferred_element_type=jnp.float32).astype(
        jnp.bfloat16
    )
    send_buffer = send_buffer.reshape(devices_gy, CAP, tile_rows * tile_cols)
    arrived = lax.all_to_all(send_buffer, "gy", split_axis=0, concat_axis=0, tiled=True).reshape(
        slot_total, tile_rows, tile_cols
    )
    ky_onehot = (
        slot_ky[:, None] == lax.broadcasted_iota(jnp.int32, (1, wy_table.shape[0]), 1)
    ).astype(jnp.bfloat16)
    vertical = jnp.einsum(
        "mk,kys->mys", ky_onehot, wy_table, preferred_element_type=jnp.float32
    ).astype(jnp.bfloat16)
    row_samples = jnp.einsum(
        "mys,msw->myw", vertical, arrived, preferred_element_type=jnp.float32
    ).astype(jnp.bfloat16)
    kx_onehot = (
        slot_kx[:, None] == lax.broadcasted_iota(jnp.int32, (1, wx_table.shape[0]), 1)
    ).astype(jnp.bfloat16)
    horizontal = jnp.einsum(
        "mk,ksp->msp", kx_onehot, wx_table, preferred_element_type=jnp.float32
    ).astype(jnp.bfloat16)
    patches = jnp.einsum(
        "myw,mwp->myp", row_samples, horizontal, preferred_element_type=jnp.float32
    )
    x_blocks = X // tile_cols
    placement = (
        (slot_z * x_blocks + slot_xb)[:, None]
        == lax.broadcasted_iota(jnp.int32, (1, Z * x_blocks), 1)
    ) & slot_live[:, None]
    rendered = jnp.einsum(
        "mq,myp->qyp", placement.astype(jnp.float32), patches, precision=lax.Precision.HIGHEST
    )
    image = (
        rendered.reshape(Z, x_blocks, YB, tile_cols)
        .transpose(0, 2, 1, 3)
        .reshape(Z, YB, X)
        .astype(jnp.bfloat16)
    )
    extended = with_halo(image[None], (("gy", 2),), 3)
    features = extended
    for weight, bias, extra_rows in (
        (w_first, b_first, 2),
        (w_second, b_second, 1),
        (w_third, b_third, 0),
    ):
        result = convolve(features, weight, bias)
        row_count = result.shape[2]
        global_row = own_index * YB - extra_rows + lax.broadcasted_iota(jnp.int32, (row_count,), 0)
        inside = (global_row >= 0) & (global_row < YB * devices_gy)
        features = jnp.where(inside[None, None, :, None], result, jnp.zeros_like(result)).astype(
            jnp.bfloat16
        )
    return features


def solution(mesh):
    return jax.shard_map(
        on_device,
        mesh=mesh,
        in_specs=(
            P(("groups", "gy"), None, None),
            P("groups", None),
            P("groups"),
            P("groups"),
            P("groups"),
            P("groups"),
            P("groups"),
            P(),
            P(),
            P(),
            P(),
            P(),
            P(),
            P(),
            P(),
        ),
        out_specs=P(None, "groups", "gy", None),
        check_vma=False,
    )
```

profile of v0, /device:TPU:15, one launch (start us, length us, event | category | flops | bytes accessed | tf_op | source)
XLA Modules:
  0.0 104.1 jit_solution(4561536459919610972)
XLA Ops:
  0.0 0.5 broadcast.173
  0.6 1.3 %reduce.3 = s32[512]{0:T(512)S(1)} reduce(s32[512,1]{0,1:T(1,128)} %param.16, s32[]{:T(128)} %broadcast.173), dimensions={1}, to_apply=%param.16.reduce_sub_computation.3 | reduce | bytes 4100 | tf_op args[1]
  1.9 0.1 reshape_squeeze.3
  2.0 0.8 reshape.144
  2.7 0.5 convert_reduce_fusion
  3.2 1.4 %convolution_convert_fusion = bf16[64,2048]{1,0:T(8,128)(2,1)S(1)} fusion(bf16[4,8,16,128]{3,2,1,0:T(8,128)(2,1)} %bitcast.62, s32[32]{0:T(128)S(1)} %get-tuple-element.17, s32[32]{0:T(128)S(1)} %get-tuple-element.16), kind=kOutput, calls=%fused_computation.33 | convolution fusion | flops 8655872 | bytes 393472 | tf_op jit(solution)/shard_map/dot_general | solution.py:103
  4.6 0.8 reshape.146
  5.5 6.6 %all-to-all-start = ((bf16[16,4,2048]{2,1,0:T(4,128)(2,1)}), bf16[16,4,2048]{2,1,0:T(4,128)(2,1)S(1)}, u32[]{:S(2)}, u32[]{:S(2)}) async-start(bf16[16,4,2048]{2,1,0:T(4,128)(2,1)} %reshape.146), calls=%async_computation | async-start | bytes 524288 | tf_op jit(solution)/shard_map/all_to_all | solution.py:107
  12.0 0.7 convert_element_type.137
  12.7 0.7 convert_element_type.140
  13.4 0.7 convert_element_type.144
  14.1 0.7 convert_element_type.152
  14.8 0.1 convert_element_type.153
  14.8 0.1 convert_element_type.145
  14.9 0.1 convert_element_type.141
  15.0 0.1 convert_element_type.138
  15.1 0.1 convert_reduce_fusion.1
  15.2 0.1 copy.41
  15.3 0.1 gt.15
  15.4 0.1 copy.40
  15.5 0.1 add.85
  15.6 0.1 copy.42
  15.7 0.1 convert_element_type.147
  15.8 0.1 copy.45
  15.9 0.1 convert_element_type.155
  16.0 0.9 convolution_convert_fusion.3
  16.9 0.1 copy.44
  17.0 0.5 compare_and_fusion.2
  17.6 0.8 convolution_convert_fusion.1
  18.4 1.6 %all-to-all-done = bf16[16,4,2048]{2,1,0:T(4,128)(2,1)S(1)} async-done(((bf16[16,4,2048]{2,1,0:T(4,128)(2,1)}), bf16[16,4,2048]{2,1,0:T(4,128)(2,1)S(1)}, u32[]{:S(2)}, u32[]{:S(2)}) %all-to-all-start) | async-done | bytes 262176 | tf_op jit(solution)/shard_map/all_to_all | solution.py:107
  20.0 0.2 reshape.147
  20.1 1.9 %fusion.36 = f32[64,8,128]{2,1,0:T(8,128)S(1)} fusion(bf16[64,128,128]{2,0,1:T(8,128)(2,1)S(1)} %convolution_convert_fusion.1, bf16[64,8,16]{2,1,0:T(8,128)(2,1)S(1)} %copy.44, bf16[64,16,128]{2,1,0:T(8,128)(2,1)S(1)} %reshape.147), kind=kOutput, calls=%fused_computation.39 | convolution fusion | flops 18939904 | bytes 2637824 | tf_op jit(solution)/shard_map/myw,mwp->myp/dot_general | solution.py:125
  22.1 0.2 convolution_convert_fusion.4
  22.4 3.7 %collective-permute-start = (bf16[1,4,3,512]{3,1,2,0:T(4,128)(2,1)S(1)}, bf16[1,4,3,512]{3,1,2,0:T(4,128)(2,1)S(1)}, u32[]{:S(2)}, u32[]{:S(2)}) collective-permute-start(bf16[1,4,3,512]{3,1,2,0:T(4,128)(2,1)S(1)} %get-tuple-element.14), channel_id=1, source_target_pairs={{0,1},{1,2},{2,3},{3,4},{4,5},{5,6},{6,7},{7,8},{8,9},{9,10},{10,1... | collective-permute-start | bytes 36872 | tf_op jit(solution)/shard_map/ppermute | solution.py:20
  26.0 2.1 %collective-permute-start.1 = (bf16[1,4,3,512]{3,1,2,0:T(4,128)(2,1)S(1)}, bf16[1,4,3,512]{3,1,2,0:T(4,128)(2,1)S(1)}, u32[]{:S(2)}, u32[]{:S(2)}) collective-permute-start(bf16[1,4,3,512]{3,1,2,0:T(4,128)(2,1)S(1)} %get-tuple-element.15), channel_id=1, source_target_pairs={{1,0},{2,1},{3,2},{4,3},{5,4},{6,5},{7,6},{8,7},{9,8},{10,9},{11,1... | collective-permute-start | bytes 36872 | tf_op jit(solution)/shard_map/ppermute | solution.py:22
  28.2 3.8 %collective-permute-done.1 = bf16[1,4,3,512]{3,1,2,0:T(4,128)(2,1)S(1)} collective-permute-done((bf16[1,4,3,512]{3,1,2,0:T(4,128)(2,1)S(1)}, bf16[1,4,3,512]{3,1,2,0:T(4,128)(2,1)S(1)}, u32[]{:S(2)}, u32[]{:S(2)}) %collective-permute-start.1) | collective-permute-done | bytes 12320 | tf_op jit(solution)/shard_map/ppermute | solution.py:22
  32.0 0.1 pad
  32.1 0.2 reshape.150
  32.3 0.1 fusion.44
  32.4 2.1 %copy.50 = bf16[1,4,14,8,67]{3,0,4,2,1:T(2,128)(2,1)S(1)} copy(bf16[1,4,14,8,67]{4,3,1,2,0:T(8,128)(2,1)S(1)} %fusion.44) | data formatting | bytes 120064 | tf_op jit(solution)/shard_map/conv_general_dilated | solution.py:30
  34.6 0.0 copy-start.3
  34.6 22.6 %select_bitcast_fusion = bf16[4,12,1,8,65,32]{5,3,4,1,0,2:T(8,128)(2,1)S(1)} fusion(f32[32]{0:T(128)S(1)} %copy-done.6, bf16[1,4,14,8,67]{3,0,4,2,1:T(2,128)(2,1)S(1)} %copy.50, pred[12]{0:T(512)(128)(4,1)S(1)} %compare_and_fusion, pred[8,65]{0,1:T(8,128)(4,1)S(1)} %copy-done.8, bf16[32,1,3,3,3]{0,4,3,2,1:T(4,128)(2,1)S(1)} %copy-done.5), kind=kOutput, calls=%fused_computation.19 | convolution fusion | flops 40734720 | bytes 1659860 | tf_op jit(solution)/shard_map/conv_general_dilated | solution.py:30
  57.3 18.6 %fusion.27 = bf16[4,10,1,8,65,32]{5,3,4,1,0,2:T(8,128)(2,1)S(1)} fusion(f32[32]{0:T(128)S(1)} %copy-done.7, pred[10]{0:T(512)(128)(4,1)S(1)} %compare_and_fusion.1, pred[8,65]{0,1:T(8,128)(4,1)S(1)} %copy-done.8, bf16[32,32,3,3,3]{1,0,4,3,2:T(8,128)(2,1)S(1)} %copy-done.3, bf16[4,12,1,7,1,32]{5,3,4,1,0,2:T(8,128)(2,1)S(1)} %get-tuple-element.11, ...), kind=kOutput, calls=%fused_computation.30 | convolution fusion | flops 970024960 | bytes 3027602 | tf_op jit(solution)/shard_map/conv_general_dilated | solution.py:30
  76.0 14.7 %fusion.17 = f32[4,8,8,65,32]{4,2,3,1,0:T(8,128)} fusion(bf16[32,32,3,3,3]{1,0,4,3,2:T(8,128)(2,1)S(1)} %copy-done.4, bf16[4,10,1,7,1,32]{5,3,4,1,0,2:T(8,128)(2,1)S(1)} %get-tuple-element.13, bf16[4,10,1,7,1,32]{5,3,4,1,0,2:T(8,128)(2,1)S(1)} %get-tuple-element.12, bf16[4,10,1,8,65,32]{5,3,4,1,0,2:T(8,128)(2,1)S(1)} %fusion.27), kind=kOutput, calls=%fused_computation.22 | convolution fusion | flops 773632000 | bytes 3552256 | tf_op jit(solution)/shard_map/conv_general_dilated | solution.py:30
  90.6 7.9 %copy.52 = f32[4,8,8,65,32]{3,2,4,1,0:T(8,128)} copy(f32[4,8,8,65,32]{4,2,3,1,0:T(8,128)} %fusion.17) | data formatting | bytes 4259840 | tf_op jit(solution)/shard_map/conv_general_dilated | solution.py:30
  98.6 3.6 %reshape.160 = f32[4,8,1,520,32]{3,4,1,0,2:T(8,128)S(1)} reshape(f32[4,8,8,65,32]{3,2,4,1,0:T(8,128)} %copy.52) | data formatting | bytes 4259840 | tf_op jit(solution)/shard_map/conv_general_dilated | solution.py:30
  102.2 0.3 fusion.35
  102.6 1.5 %copy.53 = bf16[32,4,8,512]{3,2,1,0:T(8,128)(2,1)} copy(bf16[32,4,8,512]{3,0,2,1:T(8,128)(2,1)S(1)} %fusion.35) | data formatting | bytes 2097152 | tf_op jit(solution)/shard_map/convert_element_type | solution.py:153
  (33 shorter events, 0.3 us)
Async XLA Ops:
  0.0 17.6 %copy-start = (bf16[8,128,128]{2,1,0:T(8,128)(2,1)S(1)}, bf16[8,128,128]{2,1,0:T(8,128)(2,1)}, u32[]{:S(2)}) copy-start(bf16[8,128,128]{2,1,0:T(8,128)(2,1)} %param.23) | copy-start | bytes 786436
  0.0 34.6 %copy-start.8 = (pred[8,65]{0,1:T(8,128)(4,1)S(1)}, pred[8,65]{0,1:T(8,128)(4,1)}, u32[]{:S(2)}) copy-start(pred[8,65]{0,1:T(8,128)(4,1)} %constant.60) | copy-start | bytes 1564
  0.0 34.6 %copy-start.6 = (f32[32]{0:T(128)S(1)}, f32[32]{0:T(128)}, u32[]{:S(2)}) copy-start(f32[32]{0:T(128)} %param.25) | copy-start | bytes 388
  0.0 34.6 %copy-start.5 = (bf16[32,1,3,3,3]{0,4,3,2,1:T(4,128)(2,1)S(1)}, bf16[32,1,3,3,3]{0,4,3,2,1:T(4,128)(2,1)}, u32[]{:S(2)}) copy-start(bf16[32,1,3,3,3]{0,4,3,2,1:T(4,128)(2,1)} %param.24) | copy-start | bytes 5188
  5.5 14.5 %all-to-all-start = ((bf16[16,4,2048]{2,1,0:T(4,128)(2,1)}), bf16[16,4,2048]{2,1,0:T(4,128)(2,1)S(1)}, u32[]{:S(2)}, u32[]{:S(2)}) async-start(bf16[16,4,2048]{2,1,0:T(4,128)(2,1)} %reshape.146), calls=%async_computation | async-start | bytes 524288 | tf_op jit(solution)/shard_map/all_to_all | solution.py:107
  22.4 5.8 %collective-permute-start = (bf16[1,4,3,512]{3,1,2,0:T(4,128)(2,1)S(1)}, bf16[1,4,3,512]{3,1,2,0:T(4,128)(2,1)S(1)}, u32[]{:S(2)}, u32[]{:S(2)}) collective-permute-start(bf16[1,4,3,512]{3,1,2,0:T(4,128)(2,1)S(1)} %get-tuple-element.14), channel_id=1, source_target_pairs={{0,1},{1,2},{2,3},{3,4},{4,5},{5,6},{6,7},{7,8},{8,9},{9,10},{10,1... | collective-permute-start | bytes 36872 | tf_op jit(solution)/shard_map/ppermute | solution.py:20
  26.0 5.9 %collective-permute-start.1 = (bf16[1,4,3,512]{3,1,2,0:T(4,128)(2,1)S(1)}, bf16[1,4,3,512]{3,1,2,0:T(4,128)(2,1)S(1)}, u32[]{:S(2)}, u32[]{:S(2)}) collective-permute-start(bf16[1,4,3,512]{3,1,2,0:T(4,128)(2,1)S(1)} %get-tuple-element.15), channel_id=1, source_target_pairs={{1,0},{2,1},{3,2},{4,3},{5,4},{6,5},{7,6},{8,7},{9,8},{10,9},{11,1... | collective-permute-start | bytes 36872 | tf_op jit(solution)/shard_map/ppermute | solution.py:22
  34.6 22.7 %copy-start.3 = (bf16[32,32,3,3,3]{1,0,4,3,2:T(8,128)(2,1)S(1)}, bf16[32,32,3,3,3]{1,0,4,3,2:T(8,128)(2,1)}, u32[]{:S(2)}) copy-start(bf16[32,32,3,3,3]{1,0,4,3,2:T(8,128)(2,1)} %param.26) | copy-start | bytes 165892
  34.6 22.7 %copy-start.7 = (f32[32]{0:T(128)S(1)}, f32[32]{0:T(128)}, u32[]{:S(2)}) copy-start(f32[32]{0:T(128)} %param.27) | copy-start | bytes 388
  57.3 18.7 %copy-start.4 = (bf16[32,32,3,3,3]{1,0,4,3,2:T(8,128)(2,1)S(1)}, bf16[32,32,3,3,3]{1,0,4,3,2:T(8,128)(2,1)}, u32[]{:S(2)}) copy-start(bf16[32,32,3,3,3]{1,0,4,3,2:T(8,128)(2,1)} %param.28) | copy-start | bytes 165892
  98.6 3.6 %copy-start.1 = (f32[32]{0:T(128)S(1)}, f32[32]{0:T(128)}, u32[]{:S(2)}) copy-start(f32[32]{0:T(128)} %param.29) | copy-start | bytes 388
  98.6 3.6 %copy-start.2 = (pred[8]{0:T(512)(128)(4,1)S(1)}, pred[8]{0:T(512)(128)(4,1)}, u32[]{:S(2)}) copy-start(pred[8]{0:T(512)(128)(4,1)} %compare_and_fusion.2) | copy-start | bytes 28
where the time goes:
time: 105 us; the launch traced here: 104 us
  matrix products  61.1 us (58%)
  local copies, waits for them, and re-layouts  19.2 us (18%)
  starting transfers between devices  12.3 us (12%)
  other arithmetic  5.77 us (5%)
  waiting for transfers between devices  5.39 us (5%)
    conv_general_dilated x3, matrix products, convolve(): lax.conv_general_dilated(padded[None], weight, (1, 1, 1), ((1, 1), (0, 0)...  55.9 us
    conv_general_dilated x5, local copies, waits for them, and re-layouts, convolve(): lax.conv_general_dilated(padded[None], weight, (1, 1, 1), ((1, 1), (0, 0)...  13.9 us
    all_to_all x1, starting transfers between devices, on_device(): lax.all_to_all(send_buffer, 'gy', split_axis=0, concat_axis=0, tiled=True)  6.55 us
    ppermute x1, waiting for transfers between devices, with_halo(): lax.ppermute(head, axis, [((i + 1) % count, i) for i in range(ends)])  3.78 us
    ppermute x1, starting transfers between devices, with_halo(): lax.ppermute(tail, axis, [(i, (i + 1) % count) for i in range(ends)])  3.67 us
    convert_element_type x4, other arithmetic, slot_field(): field.reshape(devices_gy, 1, per_device).astype(jnp.float32)  2.74 us
    ppermute x1, starting transfers between devices, with_halo(): lax.ppermute(head, axis, [((i + 1) % count, i) for i in range(ends)])  2.1 us
  transfers between devices with their start and end apart: 3, of which 2 were waited for; matrix products, arithmetic and copies ran while one was open for 6% of the time, Pallas kernels for 0%

commit v1 on v0

v1 whole, which is shorter than its diff:
```python
import functools

import jax
import jax.numpy as jnp
from jax import lax
from jax.experimental import pallas as pl
from jax.experimental.pallas import tpu as pltpu
from jax.sharding import PartitionSpec as P

X = 512
YB = 8
Z = 4
CAP = 4
C = 32
HALO = 3
YW = 16
ROWS = YW * CAP
LANES = 128
F32 = jnp.float32
BF16 = jnp.bfloat16


def iota(shape, dim):
    return lax.broadcasted_iota(jnp.int32, shape, dim)


def send_kernel(per, axis, dest_ref, tile_ref, ky_ref, kx_ref, tiles_ref, wy_ref, wx_ref, out_ref, wyt, count):
    bricks = count.shape[0]
    base = lax.axis_index(axis) * per
    sh = wy_ref.shape[1]
    kys, kxs = wy_ref.shape[0] // YB, wx_ref.shape[0] // LANES
    cols = tiles_ref.shape[0]
    spread = (iota((sh, cols), 0) == iota((sh, cols), 1) % sh).astype(BF16)
    wyt[...] = jnp.dot(wy_ref[...], spread, preferred_element_type=F32).reshape(kys, YB, cols)

    def clear(i, carry):
        count[i] = 0
        return carry

    lax.fori_loop(0, bricks, clear, 0)
    tile_of_col = iota((YB, cols), 1) // sh
    entry_of_lane = iota((YB, per * YB), 1) // YB
    key = jnp.zeros((YB, per * YB), jnp.int32)
    vertical, kinds = [], []
    for e in range(per):
        dest = dest_ref[0, base + e]
        rank = count[dest]
        count[dest] = rank + 1
        key = jnp.where(entry_of_lane == e, dest * (YB * CAP) + rank, key)
        vertical.append(jnp.where(tile_of_col == tile_ref[0, base + e], wyt[ky_ref[0, base + e]], 0.0))
        kinds.append(kx_ref[0, base + e])
    key = (key + CAP * (iota((YB, per * YB), 1) % YB))[:1]
    samples = jnp.dot(jnp.concatenate(vertical, axis=0).astype(BF16), tiles_ref[...], preferred_element_type=F32)
    samples = samples.astype(BF16).astype(F32)
    by_kind = []
    for k in range(kxs):
        by_kind.append(
            jnp.concatenate(
                [jnp.where(kinds[e] == k, samples[e * YB : (e + 1) * YB], 0.0) for e in range(per)], axis=0
            ).astype(BF16)
        )
    patches = jnp.dot(jnp.concatenate(by_kind, axis=1), wx_ref[...], preferred_element_type=F32).astype(BF16)
    block = 256
    for j in range(bricks * ROWS // block):
        row = j * block + iota((block, per * YB), 0)
        row_key = (row // ROWS) * (YB * CAP) + row % ROWS - HALO * CAP
        chooser = (row_key == key).astype(F32).astype(BF16)
        out_ref[j * block : (j + 1) * block] = jnp.dot(chooser, patches, preferred_element_type=F32).astype(BF16)


def banded(w_ref, out_ref):
    wide = Z * C
    lane = iota((C, wide), 1)
    zero = jnp.zeros((wide, wide), BF16)
    gap = jnp.zeros((C, wide - 3 * C), F32)
    for c in range(3):
        for b in range(3):
            taps = [w_ref[(a * 3 + b) * 3 + c].astype(F32) for a in range(3)]
            row = jnp.concatenate(taps + [gap], axis=1)
            rows = []
            for z in range(Z):
                moved = row if z == 1 else pltpu.roll(row, ((z - 1) * C) % wide, 1)
                if z == 0:
                    moved = jnp.where(lane < 2 * C, moved, 0.0)
                if z == Z - 1:
                    moved = jnp.where(lane >= (Z - 2) * C, moved, 0.0)
                rows.append(moved)
            block = jnp.concatenate(rows, axis=0).astype(BF16)
            for y in range(2):
                out_ref[c, y * wide : (y + 1) * wide, (y + b) * wide : (y + b + 1) * wide] = block
        out_ref[c, :wide, 3 * wide :] = zero
        out_ref[c, wide:, :wide] = zero


def bias_rows(b_ref):
    column = jnp.sum(
        jnp.where(iota((C, C), 0) == iota((C, C), 1), jnp.broadcast_to(b_ref[...], (C, C)), 0.0), axis=1, keepdims=True
    )
    return jnp.concatenate([jnp.broadcast_to(column, (C, LANES))] * Z, axis=0)


def prep_kernel(per, axis, dest_ref, z_ref, xb_ref, w1_ref, b1_ref, w2_ref, b2_ref, w3_ref, b3_ref,
                place_ref, m1_ref, m2_ref, m3_ref, bias_ref, taps):
    own = lax.axis_index(axis)
    banded(w2_ref, m2_ref)
    banded(w3_ref, m3_ref)
    for n, b_ref in enumerate((b1_ref, b2_ref, b3_ref)):
        bias_ref[n] = bias_rows(b_ref)
    taps[...] = jnp.zeros_like(taps)
    for ab in range(9):
        taps[ab * 4 : ab * 4 + 3, :C] = w1_ref[ab].astype(F32)
    first = jnp.transpose(taps[...])[:C].astype(BF16)
    wide1 = m1_ref.shape[1]
    t = iota((LANES, wide1), 0)
    col = iota((LANES, wide1), 1)
    t_c, t_b, t_a = t % 4, (t // 4) % 3, t // 12
    for y in range(2):
        for z in range(Z):
            z_in = z + t_a - 1
            good = (t < 36) & (t_c < 3) & (z_in >= 0) & (z_in < Z)
            pick = (good & (col == t_c * (4 * Z) + (t_b + y) * Z + z_in)).astype(F32).astype(BF16)
            at = (y * Z + z) * C
            m1_ref[at : at + C, :] = jnp.dot(first, pick, preferred_element_type=F32).astype(BF16)
    chunks, rows, wide = place_ref.shape
    earlier = (
        (iota((LANES, LANES), 0) < iota((LANES, LANES), 1))
        & (iota((LANES, LANES), 0) // per == iota((LANES, LANES), 1) // per)
    ).astype(F32).astype(BF16)
    slot_k, y_k, src_k = iota((wide, LANES), 0) % CAP, (iota((wide, LANES), 0) // CAP) % YW, iota((wide, LANES), 0) // ROWS
    same_source = src_k == iota((wide, LANES), 1) // per
    code_row = (iota((rows, LANES), 0) // ROWS) * Z + iota((rows, LANES), 0) % Z
    same_y = (iota((rows, wide), 0) // Z) % YW == (iota((rows, wide), 1) // CAP) % YW

    def one(n, carry):
        at = pl.multiple_of(n * LANES, LANES)
        dest = jnp.broadcast_to(dest_ref[:, pl.ds(at, LANES)], (8, LANES))
        code = xb_ref[:, pl.ds(at, LANES)] * Z + z_ref[:, pl.ds(at, LANES)]
        sub = iota((8, LANES), 0)
        named = (dest == own - 1 + sub) & (sub < 3)
        rank = jnp.dot(named.astype(F32).astype(BF16), earlier, preferred_element_type=F32).astype(jnp.int32)
        slot = jnp.where(named, rank, -1)
        wanted = jnp.where(y_k < HALO, slot[0:1], jnp.where(y_k < HALO + YB, slot[1:2], slot[2:3]))
        held = (same_source & (slot_k == wanted) & (y_k < YB + 2 * HALO)).astype(F32).astype(BF16)
        cell = (code_row == code).astype(F32).astype(BF16)
        hits = lax.dot_general(cell, held, (((1,), (1,)), ((), ())), preferred_element_type=F32)
        place_ref[n] = jnp.where(same_y, hits, 0.0).astype(BF16)
        return carry

    if chunks <= 8:
        for n in range(chunks):
            one(n, 0)
    else:
        lax.fori_loop(0, chunks, one, 0)


def shifted(values):
    lane = iota(values.shape, 1)
    last = values.shape[1] - 1
    return (
        jnp.where(lane == 0, 0.0, pltpu.roll(values, 1, 1)),
        values,
        jnp.where(lane == last, 0.0, pltpu.roll(values, last, 1)),
    )


def conv_kernel(axis, bricks, arrived_ref, place_ref, m1_ref, m2_ref, m3_ref, bias_ref, out_ref, g2, g3, staged):
    own = lax.axis_index(axis)
    above, below = (own > 0).astype(F32), (own < bricks - 1).astype(F32)
    chunks, rows, wide = place_ref.shape
    wide_m = Z * C

    def place(n, total):
        at = n * wide if isinstance(n, int) else pl.multiple_of(n * wide, wide)
        return total + jnp.dot(place_ref[n], arrived_ref[pl.ds(at, wide)], preferred_element_type=F32)

    total = jnp.zeros((rows, LANES), F32)
    if chunks <= 8:
        for n in range(chunks):
            total = place(n, total)
    else:
        total = lax.fori_loop(0, chunks, place, total)
    image = jnp.concatenate([total[n * ROWS : (n + 1) * ROWS] for n in range(X // LANES)], axis=1)
    image = image.astype(BF16).astype(F32)
    moved = shifted(image)

    def bias_of(n):
        return jnp.concatenate([bias_ref[n]] * (X // LANES), axis=1)

    pairs1, pairs2, pairs3 = YB // 2 + 2, YB // 2 + 1, YB // 2
    for p in range(pairs1):
        gathered = jnp.concatenate([m[2 * p * Z : (2 * p + 4) * Z] for m in moved], axis=0)
        gathered = jnp.concatenate([gathered, jnp.zeros((m1_ref.shape[1] - 12 * Z, X), F32)], axis=0).astype(BF16)
        acc = jnp.dot(m1_ref[...], gathered, preferred_element_type=F32)
        for y in range(2):
            value = jnp.maximum(acc[y * wide_m : (y + 1) * wide_m] + bias_of(0), 0.0)
            if p == 0:
                value = value * above
            if p == pairs1 - 1:
                value = value * below
            for c, v in enumerate(shifted(value)):
                g2[c, (2 * p + y) * wide_m : (2 * p + y + 1) * wide_m] = v.astype(BF16)

    def layer(m_ref, g, p):
        acc = None
        for c in range(3):
            part = jnp.dot(m_ref[c], g[c, 2 * p * wide_m : (2 * p + 4) * wide_m], preferred_element_type=F32)
            acc = part if acc is None else acc + part
        return acc

    for p in range(pairs2):
        acc = layer(m2_ref, g2, p)
        for y in range(2):
            value = jnp.maximum(acc[y * wide_m : (y + 1) * wide_m] + bias_of(1), 0.0)
            if p == 0 and y == 0:
                value = value * above
            if p == pairs2 - 1 and y == 1:
                value = value * below
            for c, v in enumerate(shifted(value)):
                g3[c, (2 * p + y) * wide_m : (2 * p + y + 1) * wide_m] = v.astype(BF16)

    for p in range(pairs3):
        acc = layer(m3_ref, g3, p)
        for y in range(2):
            staged[:, 2 * p + y, :] = jnp.maximum(acc[y * wide_m : (y + 1) * wide_m] + bias_of(2), 0.0)
    for z in range(Z):
        out_ref[:, z] = staged[z * C : (z + 1) * C].astype(BF16)


def on_device(tiles, entry_dest, entry_tile, entry_z, entry_xb, entry_ky, entry_kx, wy_table, wx_table,
              w_first, b_first, w_second, b_second, w_third, b_third):
    bricks = lax.axis_size("gy")
    entries = entry_dest.shape[0]
    per = entries // bricks
    n_tiles, sh, sw = tiles.shape
    dest = entry_dest.T
    tile, z, xb, ky, kx = (a.reshape(1, entries) for a in (entry_tile, entry_z, entry_xb, entry_ky, entry_kx))
    smem = pl.BlockSpec(memory_space=pltpu.SMEM)
    vmem = pl.BlockSpec(memory_space=pltpu.VMEM)
    kys = wy_table.shape[0]
    send = pl.pallas_call(
        functools.partial(send_kernel, per, "gy"),
        out_shape=jax.ShapeDtypeStruct((bricks * ROWS, sw), BF16),
        in_specs=[smem] * 4 + [vmem] * 3,
        out_specs=vmem,
        scratch_shapes=[pltpu.VMEM((kys, YB, n_tiles * sh), F32), pltpu.SMEM((bricks,), jnp.int32)],
        compiler_params=pltpu.CompilerParams(vmem_limit_bytes=24 * 1024 * 1024),
        name="send",
    )(dest, tile, ky, kx, tiles.reshape(n_tiles * sh, sw), wy_table.reshape(kys * YB, sh), wx_table.reshape(-1, sw))
    arrived = lax.all_to_all(send.reshape(bricks, ROWS, sw), "gy", split_axis=0, concat_axis=0, tiled=True)
    arrived = arrived.reshape(bricks * ROWS, sw)

    chunks = entries // LANES
    wide = LANES // per * ROWS
    rows = X // sw * ROWS
    w1 = w_first.transpose(1, 2, 3, 4, 0).reshape(9, 3, C)
    w2, w3 = (w.transpose(2, 3, 4, 0, 1).reshape(27, C, C) for w in (w_second, w_third))
    place, m1, m2, m3, bias = pl.pallas_call(
        functools.partial(prep_kernel, per, "gy"),
        out_shape=[
            jax.ShapeDtypeStruct((chunks, rows, wide), BF16),
            jax.ShapeDtypeStruct((2 * Z * C, 64), BF16),
            jax.ShapeDtypeStruct((3, 2 * Z * C, 4 * Z * C), BF16),
            jax.ShapeDtypeStruct((3, 2 * Z * C, 4 * Z * C), BF16),
            jax.ShapeDtypeStruct((3, Z * C, LANES), F32),
        ],
        in_specs=[vmem] * 9,
        out_specs=[vmem] * 5,
        scratch_shapes=[pltpu.VMEM((LANES, LANES), F32)],
        compiler_params=pltpu.CompilerParams(vmem_limit_bytes=24 * 1024 * 1024),
        cost_estimate=pl.CostEstimate(flops=200_000_000, bytes_accessed=3_000_000, transcendentals=0),
        name="prep",
    )(dest, z, xb, w1, b_first.reshape(1, C), w2, b_second.reshape(1, C), w3, b_third.reshape(1, C))

    return pl.pallas_call(
        functools.partial(conv_kernel, "gy", bricks),
        out_shape=jax.ShapeDtypeStruct((C, Z, YB, X), BF16),
        in_specs=[vmem] * 6,
        out_specs=vmem,
        scratch_shapes=[
            pltpu.VMEM((3, (YB + 4) * Z * C, X), BF16),
            pltpu.VMEM((3, (YB + 2) * Z * C, X), BF16),
            pltpu.VMEM((Z * C, YB, X), F32),
        ],
        compiler_params=pltpu.CompilerParams(vmem_limit_bytes=40 * 1024 * 1024),
        cost_estimate=pl.CostEstimate(flops=4_000_000_000, bytes_accessed=6_000_000, transcendentals=0),
        name="convs",
    )(arrived, place, m1, m2, m3, bias)


def solution(mesh):
    return jax.shard_map(
        on_device,
        mesh=mesh,
        in_specs=(
            P(("groups", "gy"), None, None),
            P("groups", None),
            P("groups"),
            P("groups"),
            P("groups"),
            P("groups"),
            P("groups"),
            P(),
            P(),
            P(),
            P(),
            P(),
            P(),
            P(),
            P(),
        ),
        out_specs=P(None, "groups", "gy", None),
        check_vma=False,
    )
```

time: 105 us -> 30.2 us (0.29)
  the two profiles are of different devices: /device:TPU:15 before, /device:TPU:0 now
where the time goes in v1:
time: 30.2 us; the launch traced here: 29.8 us
  Pallas kernels  10.2 us (34%)
  waiting for transfers between devices  8.01 us (27%)
  starting transfers between devices  7.53 us (25%)
  local copies, waits for them, and re-layouts  3.96 us (13%)
    all_to_all x1, waiting for transfers between devices, on_device(): lax.all_to_all(send.reshape(bricks, ROWS, sw), 'gy', split_axis=0, concat...  8.01 us
    all_to_all x1, starting transfers between devices, on_device(): lax.all_to_all(send.reshape(bricks, ROWS, sw), 'gy', split_axis=0, concat...  7.53 us
    pallas_call x1, Pallas kernels, on_device(): pl.pallas_call(functools.partial(conv_kernel, 'gy', bricks), out_shape=ja...  6.53 us
    unnamed x30, local copies, waits for them, and re-layouts  3.96 us
    pallas_call x1, Pallas kernels, on_device(): pl.pallas_call(functools.partial(send_kernel, per, 'gy'), out_shape=jax.S...  2.36 us
    pallas_call x1, Pallas kernels, on_device(): pl.pallas_call(functools.partial(prep_kernel, per, 'gy'), out_shape=[jax....  1.31 us
  transfers between devices with their start and end apart: 1, of which 1 were waited for; matrix products, arithmetic and copies ran while one was open for 0% of the time, Pallas kernels for 4%

profile of v1, /device:TPU:0, one launch (start us, length us, event | category | flops | bytes accessed | tf_op | source)
XLA Modules:
  0.0 29.8 jit_solution(4751125504505940148)
XLA Ops:
  0.0 0.0 copy-start.6
  0.0 0.0 copy-start.5
  0.0 0.0 copy-start.4
  0.0 0.0 copy-start.3
  0.0 0.7 %copy-done.6 = s32[512,1]{0,1:T(1,128)S(1)} copy-done((s32[512,1]{0,1:T(1,128)S(1)}, s32[512,1]{0,1:T(1,128)}, u32[]{:S(2)}) %copy-start.6) | copy-done | bytes 2072
  0.7 0.0 copy-done.5
  0.7 0.0 copy-done.4
  0.7 0.0 copy-done.3
  0.7 0.0 copy-start
  0.7 0.9 %copy-done = bf16[8,128,128]{2,1,0:T(8,128)(2,1)S(1)} copy-done((bf16[8,128,128]{2,1,0:T(8,128)(2,1)S(1)}, bf16[8,128,128]{2,1,0:T(8,128)(2,1)}, u32[]{:S(2)}) %copy-start) | copy-done | bytes 262168
  1.7 0.0 copy-start.1
  1.7 0.9 %copy-done.1 = bf16[32,16,128]{2,1,0:T(8,128)(2,1)S(1)} copy-done((bf16[32,16,128]{2,1,0:T(8,128)(2,1)S(1)}, bf16[32,16,128]{2,1,0:T(8,128)(2,1)}, u32[]{:S(2)}) %copy-start.1) | copy-done | bytes 131096
  2.6 0.0 copy-start.2
  2.6 0.7 %copy-done.2 = bf16[8,8,16]{2,1,0:T(8,128)(2,1)S(1)} copy-done((bf16[8,8,16]{2,1,0:T(8,128)(2,1)S(1)}, bf16[8,8,16]{2,1,0:T(8,128)(2,1)}, u32[]{:S(2)}) %copy-start.2) | copy-done | bytes 2072
  3.3 2.4 %send.1 = bf16[1024,128]{1,0:T(8,128)(2,1)} custom-call(s32[1,512]{1,0:T(1,128)S(1)} %bitcast.30, s32[1,512]{1,0:T(1,128)S(1)} %bitcast.27, s32[1,512]{1,0:T(1,128)S(1)} %bitcast.28, s32[1,512]{1,0:T(1,128)S(1)} %bitcast.29, bf16[512,128]{1,0:T(8,128)(2,1)S(1)} %bitcast.25, bf16[64,16]{1,0:T(8,128)(2,1)S(1)} %bitcast.26, bf16[1024,128]{1,0:T(8,128)(2,1)S(1)} %bitcast.24), custom_call_target="tpu_custom_call" | custom-call | tf_op jit(solution)/shard_map/send/pallas_call | solution.py:240
  5.7 0.0 copy-start.7
  5.7 0.0 copy-start.8
  5.7 0.0 copy-start.11
  5.7 7.5 %all-to-all-start = ((bf16[16,64,128]{2,1,0:T(8,128)(2,1)}), bf16[16,64,128]{2,1,0:T(8,128)(2,1)S(1)}, u32[]{:S(2)}, u32[]{:S(2)}) async-start(bf16[16,64,128]{2,1,0:T(8,128)(2,1)} %bitcast.7), calls=%async_computation | async-start | bytes 524288 | tf_op jit(solution)/shard_map/all_to_all | solution.py:249
  13.2 0.0 copy-start.9
  13.2 0.0 copy-start.10
  13.2 0.0 copy-start.12
  13.2 0.0 copy-start.13
  13.3 0.0 copy-start.14
  13.3 0.0 copy-done.7
  13.3 0.0 copy-done.8
  13.3 0.0 copy-done.11
  13.3 0.6 %copy-done.9 = bf16[32,1,3,3,3]{0,4,3,2,1:T(4,128)(2,1)S(1)} copy-done((bf16[32,1,3,3,3]{0,4,3,2,1:T(4,128)(2,1)S(1)}, bf16[32,1,3,3,3]{0,4,3,2,1:T(4,128)(2,1)}, u32[]{:S(2)}) %copy-start.9) | copy-done | bytes 1752
  13.9 0.0 copy-done.10
  13.9 0.0 copy-done.12
  13.9 0.0 copy-done.13
  13.9 0.0 copy-done.14
  13.9 1.3 %prep.1 = (bf16[4,256,256]{2,1,0:T(8,128)(2,1)S(1)}, bf16[256,64]{1,0:T(8,128)(2,1)S(1)}, bf16[3,256,512]{2,1,0:T(8,128)(2,1)S(1)}, bf16[3,256,512]{2,1,0:T(8,128)(2,1)S(1)}, f32[3,128,128]{2,1,0:T(8,128)S(1)}) custom-call(s32[1,512]{1,0:T(1,128)S(1)} %bitcast.31, s32[1,512]{1,0:T(1,128)S(1)} %bitcast.35, s32[1,512]{1,0:T(1,128)S(1)} %bitcast.36, ...), custom_call_target="tpu_custom_call" | custom-call | flops 200000000 | bytes 3000000 | tf_op jit(solution)/shard_map/prep/pallas_call | solution.py:257
  15.2 8.0 %all-to-all-done = bf16[16,64,128]{2,1,0:T(8,128)(2,1)S(1)} async-done(((bf16[16,64,128]{2,1,0:T(8,128)(2,1)}), bf16[16,64,128]{2,1,0:T(8,128)(2,1)S(1)}, u32[]{:S(2)}, u32[]{:S(2)}) %all-to-all-start) | async-done | bytes 262176 | tf_op jit(solution)/shard_map/all_to_all | solution.py:249
  23.3 6.5 %convs.1 = bf16[32,4,8,512]{3,2,1,0:T(8,128)(2,1)} custom-call(bf16[1024,128]{1,0:T(8,128)(2,1)S(1)} %bitcast.23, bf16[4,256,256]{2,1,0:T(8,128)(2,1)S(1)} %get-tuple-element.10.place_ref, bf16[256,64]{1,0:T(8,128)(2,1)S(1)} %get-tuple-element.11.m1_ref, bf16[3,256,512]{2,1,0:T(8,128)(2,1)S(1)} %get-tuple-element.12.m2_ref, ...), custom_call_target="tpu_custom_call" | custom-call | flops 4000000000 | bytes 6000000 | tf_op jit(solution)/shard_map/convs/pallas_call | solution.py:274
Async XLA Ops:
  0.0 0.7 %copy-start.6 = (s32[512,1]{0,1:T(1,128)S(1)}, s32[512,1]{0,1:T(1,128)}, u32[]{:S(2)}) copy-start(s32[512,1]{0,1:T(1,128)} %param.16) | copy-start | bytes 6148
  0.0 0.7 %copy-start.5 = (s32[512]{0:T(512)S(1)}, s32[512]{0:T(512)}, u32[]{:S(2)}) copy-start(s32[512]{0:T(512)} %param.21) | copy-start | bytes 6148
  0.0 0.7 %copy-start.4 = (s32[512]{0:T(512)S(1)}, s32[512]{0:T(512)}, u32[]{:S(2)}) copy-start(s32[512]{0:T(512)} %param.20) | copy-start | bytes 6148
  0.0 0.7 %copy-start.3 = (s32[512]{0:T(512)S(1)}, s32[512]{0:T(512)}, u32[]{:S(2)}) copy-start(s32[512]{0:T(512)} %param.17) | copy-start | bytes 6148
  0.7 0.9 %copy-start = (bf16[8,128,128]{2,1,0:T(8,128)(2,1)S(1)}, bf16[8,128,128]{2,1,0:T(8,128)(2,1)}, u32[]{:S(2)}) copy-start(bf16[8,128,128]{2,1,0:T(8,128)(2,1)} %param.23) | copy-start | bytes 786436
  1.7 0.9 %copy-start.1 = (bf16[32,16,128]{2,1,0:T(8,128)(2,1)S(1)}, bf16[32,16,128]{2,1,0:T(8,128)(2,1)}, u32[]{:S(2)}) copy-start(bf16[32,16,128]{2,1,0:T(8,128)(2,1)} %param.15) | copy-start | bytes 393220
  2.6 0.7 %copy-start.2 = (bf16[8,8,16]{2,1,0:T(8,128)(2,1)S(1)}, bf16[8,8,16]{2,1,0:T(8,128)(2,1)}, u32[]{:S(2)}) copy-start(bf16[8,8,16]{2,1,0:T(8,128)(2,1)} %param.22) | copy-start | bytes 6148
  5.7 7.6 %copy-start.7 = (bf16[32,32,3,3,3]{1,0,4,3,2:T(8,128)(2,1)S(1)}, bf16[32,32,3,3,3]{1,0,4,3,2:T(8,128)(2,1)}, u32[]{:S(2)}) copy-start(bf16[32,32,3,3,3]{1,0,4,3,2:T(8,128)(2,1)} %param.26) | copy-start | bytes 165892
  5.7 7.6 %copy-start.8 = (bf16[32,32,3,3,3]{1,0,4,3,2:T(8,128)(2,1)S(1)}, bf16[32,32,3,3,3]{1,0,4,3,2:T(8,128)(2,1)}, u32[]{:S(2)}) copy-start(bf16[32,32,3,3,3]{1,0,4,3,2:T(8,128)(2,1)} %param.28) | copy-start | bytes 165892
  5.7 7.6 %copy-start.11 = (s32[512]{0:T(512)S(1)}, s32[512]{0:T(512)}, u32[]{:S(2)}) copy-start(s32[512]{0:T(512)} %param.19) | copy-start | bytes 6148
  5.7 17.6 %all-to-all-start = ((bf16[16,64,128]{2,1,0:T(8,128)(2,1)}), bf16[16,64,128]{2,1,0:T(8,128)(2,1)S(1)}, u32[]{:S(2)}, u32[]{:S(2)}) async-start(bf16[16,64,128]{2,1,0:T(8,128)(2,1)} %bitcast.7), calls=%async_computation | async-start | bytes 524288 | tf_op jit(solution)/shard_map/all_to_all | solution.py:249
  13.2 0.7 %copy-start.9 = (bf16[32,1,3,3,3]{0,4,3,2,1:T(4,128)(2,1)S(1)}, bf16[32,1,3,3,3]{0,4,3,2,1:T(4,128)(2,1)}, u32[]{:S(2)}) copy-start(bf16[32,1,3,3,3]{0,4,3,2,1:T(4,128)(2,1)} %param.24) | copy-start | bytes 5188
  13.2 0.7 %copy-start.10 = (s32[512]{0:T(512)S(1)}, s32[512]{0:T(512)}, u32[]{:S(2)}) copy-start(s32[512]{0:T(512)} %param.18) | copy-start | bytes 6148
  13.2 0.7 %copy-start.12 = (f32[32]{0:T(128)S(1)}, f32[32]{0:T(128)}, u32[]{:S(2)}) copy-start(f32[32]{0:T(128)} %param.25) | copy-start | bytes 388
  13.2 0.7 %copy-start.13 = (f32[32]{0:T(128)S(1)}, f32[32]{0:T(128)}, u32[]{:S(2)}) copy-start(f32[32]{0:T(128)} %param.27) | copy-start | bytes 388
  13.3 0.7 %copy-start.14 = (f32[32]{0:T(128)S(1)}, f32[32]{0:T(128)}, u32[]{:S(2)}) copy-start(f32[32]{0:T(128)} %param.29) | copy-start | bytes 388

commit v2 on v1

v2 whole, which is shorter than its diff:
```python
import functools

import jax
import jax.numpy as jnp
from jax import lax
from jax.experimental import pallas as pl
from jax.experimental.pallas import tpu as pltpu
from jax.sharding import PartitionSpec as P

X = 512
YB = 8
Z = 4
CAP = 4
C = 32
HALO = 3
YW = YB + 2 * HALO
CELLS = 16 * Z
LANES = 128
F32 = jnp.float32
BF16 = jnp.bfloat16


def payload_rows(per):
    rows = YW * CAP
    return rows if LANES // per * rows % 16 == 0 else -(-rows // 16) * 16


def iota(shape, dim):
    return lax.broadcasted_iota(jnp.int32, shape, dim)


def send_kernel(per, axis, dest_hbm, tile_hbm, ky_hbm, kx_hbm, tiles_hbm, wy_hbm, wx_hbm, out_ref,
                dest_ref, tile_ref, ky_ref, kx_ref, tiles_ref, wy_ref, wx_ref, wyt, count, sems):
    sources = (dest_hbm, tile_hbm, ky_hbm, kx_hbm, wy_hbm, tiles_hbm, wx_hbm)
    targets = (dest_ref, tile_ref, ky_ref, kx_ref, wy_ref, tiles_ref, wx_ref)
    copies = [pltpu.make_async_copy(a, b, sems.at[n]) for n, (a, b) in enumerate(zip(sources, targets))]
    for copy in copies:
        copy.start()
    bricks = count.shape[0]
    rows = out_ref.shape[0] // bricks
    base = lax.axis_index(axis) * per
    sh = wy_ref.shape[1]
    kys, kxs = wy_ref.shape[0] // YB, wx_ref.shape[0] // LANES
    cols = tiles_ref.shape[0]
    spread = (iota((sh, cols), 0) == iota((sh, cols), 1) % sh).astype(BF16)
    copies[4].wait()
    wyt[...] = jnp.dot(wy_ref[...], spread, preferred_element_type=F32).reshape(kys, YB, cols)

    def clear(i, carry):
        count[i] = 0
        return carry

    lax.fori_loop(0, bricks, clear, 0)
    for copy in copies[:4]:
        copy.wait()
    tile_of_col = iota((YB, cols), 1) // sh
    entry_of_lane = iota((YB, per * YB), 1) // YB
    key = jnp.zeros((YB, per * YB), jnp.int32)
    vertical, kinds = [], []
    for e in range(per):
        dest = dest_ref[0, base + e]
        rank = count[dest]
        count[dest] = rank + 1
        key = jnp.where(entry_of_lane == e, dest * (YB * CAP) + rank, key)
        vertical.append(jnp.where(tile_of_col == tile_ref[0, base + e], wyt[ky_ref[0, base + e]], 0.0))
        kinds.append(kx_ref[0, base + e])
    key = (key + CAP * (iota((YB, per * YB), 1) % YB))[:1]
    copies[5].wait()
    samples = jnp.dot(jnp.concatenate(vertical, axis=0).astype(BF16), tiles_ref[...], preferred_element_type=F32)
    samples = samples.astype(BF16).astype(F32)
    copies[6].wait()
    by_kind = []
    for k in range(kxs):
        by_kind.append(
            jnp.concatenate(
                [jnp.where(kinds[e] == k, samples[e * YB : (e + 1) * YB], 0.0) for e in range(per)], axis=0
            ).astype(BF16)
        )
    patches = jnp.dot(jnp.concatenate(by_kind, axis=1), wx_ref[...], preferred_element_type=F32).astype(BF16)
    block = LANES
    for j in range(bricks * rows // block):
        row = j * block + iota((block, per * YB), 0)
        row_key = (row // rows) * (YB * CAP) + row % rows - HALO * CAP
        chooser = (row_key == key).astype(F32).astype(BF16)
        out_ref[j * block : (j + 1) * block] = jnp.dot(chooser, patches, preferred_element_type=F32).astype(BF16)


def banded(w_ref, out_ref):
    wide = Z * C
    lane = iota((C, wide), 1)
    gap = jnp.zeros((C, wide - 3 * C), F32)
    for c in range(3):
        for b in range(3):
            taps = [w_ref[(a * 3 + b) * 3 + c].astype(F32) for a in range(3)]
            row = jnp.concatenate(taps + [gap], axis=1)
            rows = []
            for z in range(Z):
                moved = row if z == 1 else pltpu.roll(row, ((z - 1) * C) % wide, 1)
                if z == 0:
                    moved = jnp.where(lane < 2 * C, moved, 0.0)
                if z == Z - 1:
                    moved = jnp.where(lane >= (Z - 2) * C, moved, 0.0)
                rows.append(moved)
            at = (b * 3 + c) * wide
            out_ref[:, at : at + wide] = jnp.concatenate(rows, axis=0).astype(BF16)


def bias_rows(b_ref):
    column = jnp.sum(
        jnp.where(iota((C, C), 0) == iota((C, C), 1), jnp.broadcast_to(b_ref[...], (C, C)), 0.0), axis=1, keepdims=True
    )
    return jnp.concatenate([jnp.broadcast_to(column, (C, LANES))] * Z, axis=0)


def prep_kernel(per, axis, dest_ref, z_ref, xb_ref, w1_ref, b1_ref, w2_ref, b2_ref, w3_ref, b3_ref,
                place_ref, m1_ref, m2_ref, m3_ref, bias_ref, taps):
    own = lax.axis_index(axis)
    banded(w2_ref, m2_ref)
    banded(w3_ref, m3_ref)
    for n, b_ref in enumerate((b1_ref, b2_ref, b3_ref)):
        bias_ref[n] = bias_rows(b_ref)
    taps[...] = jnp.zeros_like(taps)
    for ab in range(9):
        taps[ab * 4 : ab * 4 + 3, :C] = w1_ref[ab].astype(F32)
    first = jnp.transpose(taps[...])[:C].astype(BF16)
    wide1 = m1_ref.shape[1]
    t = iota((LANES, wide1), 0)
    col = iota((LANES, wide1), 1)
    t_c, t_b, t_a = t % 4, (t // 4) % 3, t // 12
    for y in range(2):
        for z in range(Z):
            z_in = z + t_a - 1
            good = (t < 36) & (t_c < 3) & (z_in >= 0) & (z_in < Z)
            pick = (good & (col == t_c * (4 * Z) + (t_b + y) * Z + z_in)).astype(F32).astype(BF16)
            at = (y * Z + z) * C
            m1_ref[at : at + C, :] = jnp.dot(first, pick, preferred_element_type=F32).astype(BF16)
    chunks, rows, wide = place_ref.shape
    earlier = (
        (iota((LANES, LANES), 0) < iota((LANES, LANES), 1))
        & (iota((LANES, LANES), 0) // per == iota((LANES, LANES), 1) // per)
    ).astype(F32).astype(BF16)
    sent = payload_rows(per)
    slot_k, y_k, src_k = iota((wide, LANES), 0) % CAP, iota((wide, LANES), 0) % sent // CAP, iota((wide, LANES), 0) // sent
    same_source = src_k == iota((wide, LANES), 1) // per
    code_row = (iota((rows, LANES), 0) // CELLS) * Z + iota((rows, LANES), 0) % Z
    same_y = iota((rows, wide), 0) % CELLS // Z == iota((rows, wide), 1) % sent // CAP

    def one(n, carry):
        at = pl.multiple_of(n * LANES, LANES)
        dest = jnp.broadcast_to(dest_ref[:, pl.ds(at, LANES)], (8, LANES))
        code = xb_ref[:, pl.ds(at, LANES)] * Z + z_ref[:, pl.ds(at, LANES)]
        sub = iota((8, LANES), 0)
        named = (dest == own - 1 + sub) & (sub < 3)
        rank = jnp.dot(named.astype(F32).astype(BF16), earlier, preferred_element_type=F32).astype(jnp.int32)
        slot = jnp.where(named, rank, -1)
        wanted = jnp.where(y_k < HALO, slot[0:1], jnp.where(y_k < HALO + YB, slot[1:2], slot[2:3]))
        held = (same_source & (slot_k == wanted) & (y_k < YW)).astype(F32).astype(BF16)
        cell = (code_row == code).astype(F32).astype(BF16)
        hits = lax.dot_general(cell, held, (((1,), (1,)), ((), ())), preferred_element_type=F32)
        place_ref[n] = jnp.where(same_y, hits, 0.0).astype(BF16)
        return carry

    if chunks <= 8:
        for n in range(chunks):
            one(n, 0)
    else:
        lax.fori_loop(0, chunks, one, 0)


def shifted(values):
    lane = iota(values.shape, 1)
    last = values.shape[1] - 1
    zero = jnp.zeros_like(values)
    return (
        jnp.where(lane == 0, zero, pltpu.roll(values, 1, 1)),
        values,
        jnp.where(lane == last, zero, pltpu.roll(values, last, 1)),
    )


def conv_kernel(axis, bricks, arrived_ref, place_ref, m1_ref, m2_ref, m3_ref, bias_ref, out_ref,
                g2, g3, staged, packed, sems):
    own = lax.axis_index(axis)
    above, below = (own > 0).astype(F32), (own < bricks - 1).astype(F32)
    chunks, rows, wide = place_ref.shape
    wide_m = Z * C

    def place(n, total):
        at = n * wide if isinstance(n, int) else pl.multiple_of(n * wide, wide)
        return total + jnp.dot(place_ref[n], arrived_ref[pl.ds(at, wide)], preferred_element_type=F32)

    total = jnp.zeros((rows, LANES), F32)
    if chunks <= 8:
        for n in range(chunks):
            total = place(n, total)
    else:
        total = lax.fori_loop(0, chunks, place, total)
    image = jnp.concatenate([total[n * CELLS : (n + 1) * CELLS] for n in range(X // LANES)], axis=1)
    moved = shifted(image.astype(BF16).astype(F32))

    def bias_of(n, cols):
        return jnp.concatenate([bias_ref[n]] * (cols // LANES), axis=1)

    def keep(g, row, value):
        for c, v in enumerate(shifted(value.astype(BF16))):
            at = (row * 3 + c) * wide_m
            g[at : at + wide_m] = v

    def first(p):
        gathered = jnp.concatenate([m[2 * p * Z : (2 * p + 4) * Z] for m in moved], axis=0)
        gathered = jnp.concatenate([gathered, jnp.zeros((m1_ref.shape[1] - 12 * Z, X), F32)], axis=0).astype(BF16)
        acc = jnp.dot(m1_ref[...], gathered, preferred_element_type=F32)
        for y in range(2):
            value = jnp.maximum(acc[y * wide_m : (y + 1) * wide_m] + bias_of(0, X), 0.0)
            if p == 0:
                value = value * above
            if p == YB // 2 + 1:
                value = value * below
            keep(g2, 2 * p + y, value)

    def second(y):
        window = g2[3 * y * wide_m : 3 * (y + 3) * wide_m]
        value = jnp.maximum(jnp.dot(m2_ref[...], window, preferred_element_type=F32) + bias_of(1, X), 0.0)
        if y == 0:
            value = value * above
        if y == YB + 1:
            value = value * below
        keep(g3, y, value)

    parts, cols = packed.shape[0], packed.shape[4]

    def third(h, y):
        window = g3[3 * y * wide_m : 3 * (y + 3) * wide_m, h * cols : (h + 1) * cols]
        acc = jnp.dot(m3_ref[...], window, preferred_element_type=F32)
        staged[h, :, y, :] = jnp.maximum(acc + bias_of(2, cols), 0.0)

    def pack(h, z):
        packed[h, :, z] = staged[h, z * C : (z + 1) * C].astype(BF16)

    def send(h):
        return pltpu.make_async_copy(packed.at[h], out_ref.at[:, :, :, pl.ds(h * cols, cols)], sems.at[h])

    for p in range(YB // 2 + 2):
        first(p)
    for y in range(YB + 2):
        second(y)
    for h in range(parts):
        for y in range(YB):
            third(h, y)
        for z in range(Z):
            pack(h, z)
        send(h).start()
    for h in range(parts):
        send(h).wait()


def on_device(tiles, entry_dest, entry_tile, entry_z, entry_xb, entry_ky, entry_kx, wy_table, wx_table,
              w_first, b_first, w_second, b_second, w_third, b_third):
    bricks = lax.axis_size("gy")
    entries = entry_dest.shape[0]
    per = entries // bricks
    n_tiles, sh, sw = tiles.shape
    dest = entry_dest.T
    tile, z, xb, ky, kx = (a.reshape(1, entries) for a in (entry_tile, entry_z, entry_xb, entry_ky, entry_kx))
    hbm = pl.BlockSpec(memory_space=pl.ANY)
    vmem = pl.BlockSpec(memory_space=pltpu.VMEM)
    kys = wy_table.shape[0]
    sent = payload_rows(per)
    send = pl.pallas_call(
        functools.partial(send_kernel, per, "gy"),
        out_shape=jax.ShapeDtypeStruct((bricks * sent, sw), BF16),
        in_specs=[hbm] * 7,
        out_specs=vmem,
        scratch_shapes=[pltpu.SMEM((1, entries), jnp.int32)] * 4
        + [
            pltpu.VMEM((n_tiles * sh, sw), BF16),
            pltpu.VMEM((kys * YB, sh), BF16),
            pltpu.VMEM((wx_table.shape[0] * sw, sw), BF16),
            pltpu.VMEM((kys, YB, n_tiles * sh), F32),
            pltpu.SMEM((bricks,), jnp.int32),
            pltpu.SemaphoreType.DMA((7,)),
        ],
        compiler_params=pltpu.CompilerParams(vmem_limit_bytes=60 * 1024 * 1024),
        name="send",
    )(dest, tile, ky, kx, tiles.reshape(n_tiles * sh, sw), wy_table.reshape(kys * YB, sh), wx_table.reshape(-1, sw))
    arrived = lax.all_to_all(send.reshape(bricks, sent, sw), "gy", split_axis=0, concat_axis=0, tiled=True)
    arrived = arrived.reshape(bricks * sent, sw)

    chunks = entries // LANES
    wide = LANES // per * sent
    rows = X // sw * CELLS
    parts = 2
    w1 = w_first.transpose(1, 2, 3, 4, 0).reshape(9, 3, C)
    w2, w3 = (w.transpose(2, 3, 4, 0, 1).reshape(27, C, C) for w in (w_second, w_third))
    place, m1, m2, m3, bias = pl.pallas_call(
        functools.partial(prep_kernel, per, "gy"),
        out_shape=[
            jax.ShapeDtypeStruct((chunks, rows, wide), BF16),
            jax.ShapeDtypeStruct((2 * Z * C, 64), BF16),
            jax.ShapeDtypeStruct((Z * C, 9 * Z * C), BF16),
            jax.ShapeDtypeStruct((Z * C, 9 * Z * C), BF16),
            jax.ShapeDtypeStruct((3, Z * C, LANES), F32),
        ],
        in_specs=[vmem] * 9,
        out_specs=[vmem] * 5,
        scratch_shapes=[pltpu.VMEM((LANES, LANES), F32)],
        compiler_params=pltpu.CompilerParams(vmem_limit_bytes=24 * 1024 * 1024),
        cost_estimate=pl.CostEstimate(flops=200_000_000, bytes_accessed=3_000_000, transcendentals=0),
        name="prep",
    )(dest, z, xb, w1, b_first.reshape(1, C), w2, b_second.reshape(1, C), w3, b_third.reshape(1, C))

    return pl.pallas_call(
        functools.partial(conv_kernel, "gy", bricks),
        out_shape=jax.ShapeDtypeStruct((C, Z, YB, X), BF16),
        in_specs=[vmem] * 6,
        out_specs=pl.BlockSpec(memory_space=pl.ANY),
        scratch_shapes=[
            pltpu.VMEM((3 * (YB + 4) * Z * C, X), BF16),
            pltpu.VMEM((3 * (YB + 2) * Z * C, X), BF16),
            pltpu.VMEM((parts, Z * C, YB, X // parts), F32),
            pltpu.VMEM((parts, C, Z, YB, X // parts), BF16),
            pltpu.SemaphoreType.DMA((parts,)),
        ],
        compiler_params=pltpu.CompilerParams(vmem_limit_bytes=40 * 1024 * 1024),
        cost_estimate=pl.CostEstimate(flops=4_000_000_000, bytes_accessed=6_000_000, transcendentals=0),
        name="convs",
    )(arrived, place, m1, m2, m3, bias)


def solution(mesh):
    return jax.shard_map(
        on_device,
        mesh=mesh,
        in_specs=(
            P(("groups", "gy"), None, None),
            P("groups", None),
            P("groups"),
            P("groups"),
            P("groups"),
            P("groups"),
            P("groups"),
            P(),
            P(),
            P(),
            P(),
            P(),
            P(),
            P(),
            P(),
        ),
        out_specs=P(None, "groups", "gy", None),
        check_vma=False,
    )
```

time: 30.2 us -> 26 us (0.86)
  local copies, waits for them, and re-layouts: 3.96 us -> 0.68 us
  waiting for transfers between devices: 8.01 us -> 7.41 us
    unnamed x30 -> x18, local copies, waits for them, and re-layouts: 3.96 us -> 0.68 us
    pallas_call x1, Pallas kernels: 6.53 us -> 5.73 us  [on_device(): pl.pallas_call(functools.partial(conv_kernel, 'gy', bricks), out_shape=ja...]
    all_to_all x1, waiting for transfers between devices: 8.01 us -> 7.41 us  [on_device(): lax.all_to_all(send.reshape(bricks, sent, sw), 'gy', split_axis=0, concat...]
    pallas_call x1, Pallas kernels: 2.36 us -> 2.85 us  [on_device(): pl.pallas_call(functools.partial(send_kernel, per, 'gy'), out_shape=jax.S...]
  transfers between devices with their start and end apart: 1 -> 1, of which waited for: 1 -> 1; matrix products, arithmetic and copies ran while one was open for 0% -> 0% of each run, Pallas kernels for 4% -> 5%
where the time goes in v2:
time: 26 us; the launch traced here: 25.7 us
  Pallas kernels  9.95 us (38%)
  starting transfers between devices  7.52 us (29%)
  waiting for transfers between devices  7.41 us (28%)
  local copies, waits for them, and re-layouts  0.68 us (3%)
    all_to_all x1, starting transfers between devices, on_device(): lax.all_to_all(send.reshape(bricks, sent, sw), 'gy', split_axis=0, concat...  7.52 us
    all_to_all x1, waiting for transfers between devices, on_device(): lax.all_to_all(send.reshape(bricks, sent, sw), 'gy', split_axis=0, concat...  7.41 us
    pallas_call x1, Pallas kernels, on_device(): pl.pallas_call(functools.partial(conv_kernel, 'gy', bricks), out_shape=ja...  5.73 us
    pallas_call x1, Pallas kernels, on_device(): pl.pallas_call(functools.partial(send_kernel, per, 'gy'), out_shape=jax.S...  2.85 us
    pallas_call x1, Pallas kernels, on_device(): pl.pallas_call(functools.partial(prep_kernel, per, 'gy'), out_shape=[jax....  1.37 us
    unnamed x18, local copies, waits for them, and re-layouts  0.68 us
  transfers between devices with their start and end apart: 1, of which 1 were waited for; matrix products, arithmetic and copies ran while one was open for 0% of the time, Pallas kernels for 5%

profile of v2, /device:TPU:0, one launch (start us, length us, event | category | flops | bytes accessed | tf_op | source)
XLA Modules:
  0.0 25.7 jit_solution(16324494660507877008)
XLA Ops:
  0.0 2.8 %send.1 = bf16[896,128]{1,0:T(8,128)(2,1)} custom-call(s32[1,512]{1,0:T(1,128)} %bitcast.24, s32[1,512]{1,0:T(1,128)} %bitcast.38, s32[1,512]{1,0:T(1,128)} %bitcast.39, s32[1,512]{1,0:T(1,128)} %bitcast.40, bf16[512,128]{1,0:T(8,128)(2,1)} %bitcast.36, bf16[64,16]{1,0:T(8,128)(2,1)} %bitcast.37, bf16[1024,128]{1,0:T(8,128)(2,1)} %bitcast.35), custom_call_target="tpu_custom_call" | custom-call | tf_op jit(solution)/shard_map/send/pallas_call | solution.py:269
  2.9 0.0 copy-start.1
  2.9 0.0 copy-start.2
  2.9 0.0 copy-start.6
  2.9 0.0 copy-start.7
  2.9 0.0 copy-start.8
  2.9 7.5 %all-to-all-start = ((bf16[16,56,128]{2,1,0:T(8,128)(2,1)}), bf16[16,56,128]{2,1,0:T(8,128)(2,1)S(1)}, u32[]{:S(2)}, u32[]{:S(2)}) async-start(bf16[16,56,128]{2,1,0:T(8,128)(2,1)} %bitcast.34), calls=%async_computation | async-start | bytes 458752 | tf_op jit(solution)/shard_map/all_to_all | solution.py:286
  10.4 0.0 copy-start.3
  10.5 0.0 copy-start.4
  10.5 0.0 copy-start.5
  10.5 0.0 copy-start
  10.5 0.0 copy-done.1
  10.5 0.0 copy-done.2
  10.5 0.0 copy-done.6
  10.5 0.0 copy-done.7
  10.5 0.0 copy-done.8
  10.5 0.6 %copy-done.3 = bf16[32,1,3,3,3]{0,4,3,2,1:T(4,128)(2,1)S(1)} copy-done((bf16[32,1,3,3,3]{0,4,3,2,1:T(4,128)(2,1)S(1)}, bf16[32,1,3,3,3]{0,4,3,2,1:T(4,128)(2,1)}, u32[]{:S(2)}) %copy-start.3) | copy-done | bytes 1752
  11.2 0.0 copy-done.4
  11.2 0.0 copy-done.5
  11.2 0.0 copy-done
  11.2 1.4 %prep.1 = (bf16[4,256,224]{2,1,0:T(8,128)(2,1)S(1)}, bf16[256,64]{1,0:T(8,128)(2,1)S(1)}, bf16[128,1152]{1,0:T(8,128)(2,1)S(1)}, bf16[128,1152]{1,0:T(8,128)(2,1)S(1)}, f32[3,128,128]{2,1,0:T(8,128)S(1)}) custom-call(s32[1,512]{1,0:T(1,128)S(1)} %bitcast.25, s32[1,512]{1,0:T(1,128)S(1)} %bitcast.29, s32[1,512]{1,0:T(1,128)S(1)} %bitcast.30, ...), custom_call_target="tpu_custom_call" | custom-call | flops 200000000 | bytes 3000000 | tf_op jit(solution)/shard_map/prep/pallas_call | solution.py:295
  12.6 7.4 %all-to-all-done = bf16[16,56,128]{2,1,0:T(8,128)(2,1)S(1)} async-done(((bf16[16,56,128]{2,1,0:T(8,128)(2,1)}), bf16[16,56,128]{2,1,0:T(8,128)(2,1)S(1)}, u32[]{:S(2)}, u32[]{:S(2)}) %all-to-all-start) | async-done | bytes 229408 | tf_op jit(solution)/shard_map/all_to_all | solution.py:286
  20.0 5.7 %convs.1 = bf16[32,4,8,512]{3,2,1,0:T(8,128)(2,1)} custom-call(bf16[896,128]{1,0:T(8,128)(2,1)S(1)} %bitcast.23, bf16[4,256,224]{2,1,0:T(8,128)(2,1)S(1)} %get-tuple-element.10.place_ref, bf16[256,64]{1,0:T(8,128)(2,1)S(1)} %get-tuple-element.11.m1_ref, bf16[128,1152]{1,0:T(8,128)(2,1)S(1)} %get-tuple-element.12.m2_ref, ...), custom_call_target="tpu_custom_call" | custom-call | flops 4000000000 | bytes 6000000 | tf_op jit(solution)/shard_map/convs/pallas_call | solution.py:312
Async XLA Ops:
  2.9 7.6 %copy-start.1 = (bf16[32,32,3,3,3]{1,0,4,3,2:T(8,128)(2,1)S(1)}, bf16[32,32,3,3,3]{1,0,4,3,2:T(8,128)(2,1)}, u32[]{:S(2)}) copy-start(bf16[32,32,3,3,3]{1,0,4,3,2:T(8,128)(2,1)} %param.26) | copy-start | bytes 165892
  2.9 7.6 %copy-start.2 = (bf16[32,32,3,3,3]{1,0,4,3,2:T(8,128)(2,1)S(1)}, bf16[32,32,3,3,3]{1,0,4,3,2:T(8,128)(2,1)}, u32[]{:S(2)}) copy-start(bf16[32,32,3,3,3]{1,0,4,3,2:T(8,128)(2,1)} %param.28) | copy-start | bytes 165892
  2.9 7.6 %copy-start.6 = (f32[32]{0:T(128)S(1)}, f32[32]{0:T(128)}, u32[]{:S(2)}) copy-start(f32[32]{0:T(128)} %param.25) | copy-start | bytes 388
  2.9 7.6 %copy-start.7 = (f32[32]{0:T(128)S(1)}, f32[32]{0:T(128)}, u32[]{:S(2)}) copy-start(f32[32]{0:T(128)} %param.27) | copy-start | bytes 388
  2.9 7.6 %copy-start.8 = (f32[32]{0:T(128)S(1)}, f32[32]{0:T(128)}, u32[]{:S(2)}) copy-start(f32[32]{0:T(128)} %param.29) | copy-start | bytes 388
  2.9 17.1 %all-to-all-start = ((bf16[16,56,128]{2,1,0:T(8,128)(2,1)}), bf16[16,56,128]{2,1,0:T(8,128)(2,1)S(1)}, u32[]{:S(2)}, u32[]{:S(2)}) async-start(bf16[16,56,128]{2,1,0:T(8,128)(2,1)} %bitcast.34), calls=%async_computation | async-start | bytes 458752 | tf_op jit(solution)/shard_map/all_to_all | solution.py:286
  10.4 0.7 %copy-start.3 = (bf16[32,1,3,3,3]{0,4,3,2,1:T(4,128)(2,1)S(1)}, bf16[32,1,3,3,3]{0,4,3,2,1:T(4,128)(2,1)}, u32[]{:S(2)}) copy-start(bf16[32,1,3,3,3]{0,4,3,2,1:T(4,128)(2,1)} %param.24) | copy-start | bytes 5188
  10.5 0.7 %copy-start.4 = (s32[512]{0:T(512)S(1)}, s32[512]{0:T(512)}, u32[]{:S(2)}) copy-start(s32[512]{0:T(512)} %param.18) | copy-start | bytes 6148
  10.5 0.7 %copy-start.5 = (s32[512]{0:T(512)S(1)}, s32[512]{0:T(512)}, u32[]{:S(2)}) copy-start(s32[512]{0:T(512)} %param.19) | copy-start | bytes 6148
  10.5 0.7 %copy-start = (s32[512,1]{0,1:T(1,128)S(1)}, s32[512,1]{0,1:T(1,128)}, u32[]{:S(2)}) copy-start(s32[512,1]{0,1:T(1,128)} %param.16) | copy-start | bytes 6148

commit v3 on v2

--- a/solution.py
+++ b/solution.py
@@ -30,79 +30,88 @@
 
 
 def send_kernel(per, axis, dest_hbm, tile_hbm, ky_hbm, kx_hbm, tiles_hbm, wy_hbm, wx_hbm, out_ref,
-                dest_ref, tile_ref, ky_ref, kx_ref, tiles_ref, wy_ref, wx_ref, wyt, count, sems):
+                dest_ref, tile_ref, ky_ref, kx_ref, tiles_ref, wy_ref, wx_ref, wyt, sorted_by, placed, count, sems):
     sources = (dest_hbm, tile_hbm, ky_hbm, kx_hbm, wy_hbm, tiles_hbm, wx_hbm)
     targets = (dest_ref, tile_ref, ky_ref, kx_ref, wy_ref, tiles_ref, wx_ref)
     copies = [pltpu.make_async_copy(a, b, sems.at[n]) for n, (a, b) in enumerate(zip(sources, targets))]
     for copy in copies:
         copy.start()
+
     bricks = count.shape[0]
     rows = out_ref.shape[0] // bricks
     base = lax.axis_index(axis) * per
     sh = wy_ref.shape[1]
-    kys, kxs = wy_ref.shape[0] // YB, wx_ref.shape[0] // LANES
-    cols = tiles_ref.shape[0]
-    spread = (iota((sh, cols), 0) == iota((sh, cols), 1) % sh).astype(BF16)
-    copies[4].wait()
-    wyt[...] = jnp.dot(wy_ref[...], spread, preferred_element_type=F32).reshape(kys, YB, cols)
+    kys, fold = wy_ref.shape[0] // YB, sorted_by.shape[0]
+
+    def blank(k, carry):
+        sorted_by[k] = jnp.zeros(sorted_by.shape[1:], F32)
+        return carry
 
     def clear(i, carry):
         count[i] = 0
         return carry
 
-    lax.fori_loop(0, bricks, clear, 0)
+    def blank_placed(k, carry):
+        placed[pl.ds(pl.multiple_of(k * rows, 8), rows)] = jnp.zeros((rows, placed.shape[1]), F32)
+        return carry
+
+    lax.fori_loop(0, sorted_by.shape[0], blank, 0)
+    lax.fori_loop(0, bricks + 2, blank_placed, 0)
+    lax.fori_loop(0, count.shape[0], clear, 0)
+    group = min(per, 16)
+    copies[4].wait()
+    spread = (iota((sh, group * sh), 0) == iota((sh, group * sh), 1) % sh).astype(F32).astype(BF16)
+    wyt[...] = jnp.dot(wy_ref[...], spread, preferred_element_type=F32).reshape(kys, YB, group * sh)
     for copy in copies[:4]:
         copy.wait()
-    tile_of_col = iota((YB, cols), 1) // sh
-    entry_of_lane = iota((YB, per * YB), 1) // YB
-    key = jnp.zeros((YB, per * YB), jnp.int32)
-    vertical, kinds = [], []
+    entry_of_col = iota((YB, group * sh), 1) // sh
+    vertical = [jnp.where(entry_of_col == e % group, wyt[ky_ref[0, base + e]], 0.0) for e in range(per)]
+    copies[5].wait()
+    for g in range(0, per, group):
+        picked = [tiles_ref[pl.ds(pl.multiple_of(tile_ref[0, base + e] * sh, sh), sh)] for e in range(g, g + group)]
+        weights = jnp.concatenate(vertical[g : g + group], axis=0).astype(BF16)
+        samples = jnp.dot(weights, jnp.concatenate(picked, axis=0), preferred_element_type=F32)
+        samples = samples.astype(BF16).astype(F32)
+        for e in range(g, g + group):
+            sorted_by[kx_ref[0, base + e] % fold, e * YB : (e + 1) * YB] = samples[(e - g) * YB : (e - g + 1) * YB]
+    copies[6].wait()
+    by_kind = jnp.concatenate([sorted_by[k].astype(BF16) for k in range(fold)], axis=1)
+    sides = [wx_ref[: fold * LANES], wx_ref[fold * LANES :]]
+    patches = jnp.dot(by_kind, jnp.concatenate(sides, axis=1), preferred_element_type=F32)
     for e in range(per):
         dest = dest_ref[0, base + e]
         rank = count[dest]
         count[dest] = rank + 1
-        key = jnp.where(entry_of_lane == e, dest * (YB * CAP) + rank, key)
-        vertical.append(jnp.where(tile_of_col == tile_ref[0, base + e], wyt[ky_ref[0, base + e]], 0.0))
-        kinds.append(kx_ref[0, base + e])
-    key = (key + CAP * (iota((YB, per * YB), 1) % YB))[:1]
-    copies[5].wait()
-    samples = jnp.dot(jnp.concatenate(vertical, axis=0).astype(BF16), tiles_ref[...], preferred_element_type=F32)
-    samples = samples.astype(BF16).astype(F32)
-    copies[6].wait()
-    by_kind = []
-    for k in range(kxs):
-        by_kind.append(
-            jnp.concatenate(
-                [jnp.where(kinds[e] == k, samples[e * YB : (e + 1) * YB], 0.0) for e in range(per)], axis=0
-            ).astype(BF16)
-        )
-    patches = jnp.dot(jnp.concatenate(by_kind, axis=1), wx_ref[...], preferred_element_type=F32).astype(BF16)
-    block = LANES
-    for j in range(bricks * rows // block):
-        row = j * block + iota((block, per * YB), 0)
-        row_key = (row // rows) * (YB * CAP) + row % rows - HALO * CAP
-        chooser = (row_key == key).astype(F32).astype(BF16)
-        out_ref[j * block : (j + 1) * block] = jnp.dot(chooser, patches, preferred_element_type=F32).astype(BF16)
-
-
-def banded(w_ref, out_ref):
-    wide = Z * C
-    lane = iota((C, wide), 1)
-    gap = jnp.zeros((C, wide - 3 * C), F32)
-    for c in range(3):
-        for b in range(3):
-            taps = [w_ref[(a * 3 + b) * 3 + c].astype(F32) for a in range(3)]
-            row = jnp.concatenate(taps + [gap], axis=1)
-            rows = []
-            for z in range(Z):
-                moved = row if z == 1 else pltpu.roll(row, ((z - 1) * C) % wide, 1)
-                if z == 0:
-                    moved = jnp.where(lane < 2 * C, moved, 0.0)
-                if z == Z - 1:
-                    moved = jnp.where(lane >= (Z - 2) * C, moved, 0.0)
-                rows.append(moved)
-            at = (b * 3 + c) * wide
-            out_ref[:, at : at + wide] = jnp.concatenate(rows, axis=0).astype(BF16)
+        at = (dest + 1) * rows + rank
+        patch = patches[e * YB : (e + 1) * YB]
+        patch = jnp.where(kx_ref[0, base + e] < fold, patch[:, :LANES], patch[:, LANES:])
+        placed[pl.ds(at + HALO * CAP, YB, stride=CAP)] = patch
+        placed[pl.ds(at + rows, HALO, stride=CAP)] = patch[YB - HALO :]
+        placed[pl.ds(at - rows + (HALO + YB) * CAP, HALO, stride=CAP)] = patch[:HALO]
+    out_ref[...] = placed[rows : rows + out_ref.shape[0]].astype(BF16)
+
+
+def banded(w_ref, out_ref, rest_ref):
+    hole = jnp.zeros((C, C), F32)
+
+    def tap(a, b, c):
+        return w_ref[(a * 3 + b) * 3 + c].astype(F32)
+
+    for b in range(3):
+        taps = [[tap(a, b, c) for a in range(3)] for c in range(3)]
+        far = [piece for p in taps for piece in (p[1], p[2])]
+        near = [piece for p in taps for piece in (p[0], p[1])]
+        uppers = (far + [hole, hole], near + [taps[0][2], taps[1][2]])
+        lowers = (far + [taps[0][0], taps[1][0]], near + [hole, hole])
+        for n, rows in enumerate((uppers, lowers)):
+            block = jnp.concatenate([jnp.concatenate(row, axis=1) for row in rows], axis=0)
+            out_ref[n, b * 2 * C : (b + 1) * 2 * C] = block.astype(BF16)
+    for y in range(6):
+        reach = [r - y + 2 for r in range(4)]
+        one = [piece for b in reach for piece in (tap(2, b, 2) if 0 <= b <= 2 else hole, hole)]
+        two = [piece for b in reach for piece in (hole, tap(0, b, 2) if 0 <= b <= 2 else hole)]
+        block = jnp.concatenate([jnp.concatenate(one, axis=1), jnp.concatenate(two, axis=1)], axis=0)
+        rest_ref[y * 2 * C : (y + 1) * 2 * C] = block.astype(BF16)
 
 
 def bias_rows(b_ref):
@@ -113,10 +122,10 @@
 
 
 def prep_kernel(per, axis, dest_ref, z_ref, xb_ref, w1_ref, b1_ref, w2_ref, b2_ref, w3_ref, b3_ref,
-                place_ref, m1_ref, m2_ref, m3_ref, bias_ref, taps):
+                place_ref, m1_ref, m2_ref, r2_ref, m3_ref, r3_ref, bias_ref, taps):
     own = lax.axis_index(axis)
-    banded(w2_ref, m2_ref)
-    banded(w3_ref, m3_ref)
+    banded(w2_ref, m2_ref, r2_ref)
+    banded(w3_ref, m3_ref, r3_ref)
     for n, b_ref in enumerate((b1_ref, b2_ref, b3_ref)):
         bias_ref[n] = bias_rows(b_ref)
     taps[...] = jnp.zeros_like(taps)
@@ -178,12 +187,12 @@
     )
 
 
-def conv_kernel(axis, bricks, arrived_ref, place_ref, m1_ref, m2_ref, m3_ref, bias_ref, out_ref,
-                g2, g3, staged, packed, sems):
+def conv_kernel(axis, bricks, arrived_ref, place_ref, m1_ref, m2_ref, r2_ref, m3_ref, r3_ref, bias_ref, out_ref,
+                g2, e2, g3, e3, staged, packed, sems):
     own = lax.axis_index(axis)
     above, below = (own > 0).astype(F32), (own < bricks - 1).astype(F32)
     chunks, rows, wide = place_ref.shape
-    wide_m = Z * C
+    wide_m, half = Z * C, Z * C // 2
 
     def place(n, total):
         at = n * wide if isinstance(n, int) else pl.multiple_of(n * wide, wide)
@@ -201,10 +210,17 @@
     def bias_of(n, cols):
         return jnp.concatenate([bias_ref[n]] * (cols // LANES), axis=1)
 
-    def keep(g, row, value):
+    def keep(g, e, row, value):
+        at = 8 * C * row
         for c, v in enumerate(shifted(value.astype(BF16))):
-            at = (row * 3 + c) * wide_m
-            g[at : at + wide_m] = v
+            g[0, at + c * half : at + (c + 1) * half] = v[:half]
+            g[1, at + c * half : at + (c + 1) * half] = v[half:]
+            if c < 2:
+                g[0, at + (6 + c) * C : at + (7 + c) * C] = v[2 * C : 3 * C]
+                g[1, at + (6 + c) * C : at + (7 + c) * C] = v[C : 2 * C]
+            else:
+                e[row * half : row * half + C] = v[2 * C : 3 * C]
+                e[row * half + C : (row + 1) * half] = v[C : 2 * C]
 
     def first(p):
         gathered = jnp.concatenate([m[2 * p * Z : (2 * p + 4) * Z] for m in moved], axis=0)
@@ -216,42 +232,81 @@
                 value = value * above
             if p == YB // 2 + 1:
                 value = value * below
-            keep(g2, 2 * p + y, value)
-
-    def second(y):
-        window = g2[3 * y * wide_m : 3 * (y + 3) * wide_m]
-        value = jnp.maximum(jnp.dot(m2_ref[...], window, preferred_element_type=F32) + bias_of(1, X), 0.0)
+            keep(g2, e2, 2 * p + y, value)
+
+    def layer(m_ref, r_ref, g, e, rows_in, at, cols, finish):
+        sums = {y: [] for y in range(rows_in - 2)}
+        there = slice(at, at + cols)
+
+        def rest(r):
+            count = min(4, rows_in - r)
+            low, high = max(0, r - 2), min(rows_in - 2, r + count)
+            taps = slice((low - r + 2) * half, (high - r + 2) * half)
+            found = jnp.dot(r_ref[taps, : count * half], e[r * half : (r + count) * half, there], preferred_element_type=F32)
+            for y in range(low, high):
+                sums[y].append((C, found[(y - low) * half : (y - low + 1) * half]))
+
+        for r in range(rows_in):
+            if r % 4 == 0:
+                rest(r)
+            low, high = max(0, r - rows_in + 3), min(2, r)
+            taps = slice(low * half, (high + 1) * half)
+            window = slice(8 * C * r, 8 * C * (r + 1))
+            for n in range(2):
+                found = jnp.dot(m_ref[n, taps], g[n, window, there], preferred_element_type=F32)
+                for b in range(low, high + 1):
+                    sums[r - b].append((n * half, found[(b - low) * half : (b - low + 1) * half]))
+            if r >= 2:
+                pieces = []
+                for z in range(Z):
+                    parts_z = [v[z * C - o : z * C - o + C] for o, v in sums[r - 2] if o <= z * C < o + half]
+                    pieces.append(functools.reduce(lambda p, q: p + q, parts_z))
+                finish(r - 2, jnp.concatenate(pieces, axis=0))
+
+    def second(y, total):
+        value = jnp.maximum(total + bias_of(1, X), 0.0)
         if y == 0:
             value = value * above
         if y == YB + 1:
             value = value * below
-        keep(g3, y, value)
+        keep(g3, e3, y, value)
 
     parts, cols = packed.shape[0], packed.shape[4]
 
-    def third(h, y):
-        window = g3[3 * y * wide_m : 3 * (y + 3) * wide_m, h * cols : (h + 1) * cols]
-        acc = jnp.dot(m3_ref[...], window, preferred_element_type=F32)
-        staged[h, :, y, :] = jnp.maximum(acc + bias_of(2, cols), 0.0)
+    def third(h, y, total):
+        value = jnp.maximum(total + bias_of(2, cols), 0.0)
+        for k in range(cols // LANES):
+            staged[h, k, pl.ds(y, wide_m, stride=YB), :] = value[:, k * LANES : (k + 1) * LANES]
+        if h > 0 and y == YB // 2 - 1:
+            flush(h - 1)
 
     def pack(h, z):
-        packed[h, :, z] = staged[h, z * C : (z + 1) * C].astype(BF16)
-
-    def send(h):
-        return pltpu.make_async_copy(packed.at[h], out_ref.at[:, :, :, pl.ds(h * cols, cols)], sems.at[h])
+        for k in range(cols // LANES):
+            turned = staged[h, k, z * C * YB : (z + 1) * C * YB].astype(BF16).reshape(C, YB, LANES)
+            packed[h, z, :, :, k * LANES : (k + 1) * LANES] = turned
+
+    def send(h, z):
+        there = out_ref.at[:, z, :, pl.ds(h * cols, cols)]
+        return pltpu.make_async_copy(packed.at[h, z], there, sems.at[h, z])
 
     for p in range(YB // 2 + 2):
         first(p)
-    for y in range(YB + 2):
-        second(y)
-    for h in range(parts):
-        for y in range(YB):
-            third(h, y)
+    def flush(h):
         for z in range(Z):
             pack(h, z)
-        send(h).start()
+            send(h, z).start()
+
+    layer(m2_ref, r2_ref, g2, e2, YB + 4, 0, X, second)
     for h in range(parts):
-        send(h).wait()
+        layer(m3_ref, r3_ref, g3, e3, YB + 2, h * cols, cols, functools.partial(third, h))
+
+    @pl.when(own >= 0)
+    def _():
+        flush(parts - 1)
+
+    for h in range(parts):
+        for z in range(Z):
+            send(h, z).wait()
 
 
 def on_device(tiles, entry_dest, entry_tile, entry_z, entry_xb, entry_ky, entry_kx, wy_table, wx_table,
@@ -276,7 +331,9 @@
             pltpu.VMEM((n_tiles * sh, sw), BF16),
             pltpu.VMEM((kys * YB, sh), BF16),
             pltpu.VMEM((wx_table.shape[0] * sw, sw), BF16),
-            pltpu.VMEM((kys, YB, n_tiles * sh), F32),
+            pltpu.VMEM((kys, YB, min(per, 16) * sh), F32),
+            pltpu.VMEM((wx_table.shape[0] // 2, per * YB, sw), F32),
+            pltpu.VMEM(((bricks + 2) * sent, sw), F32),
             pltpu.SMEM((bricks,), jnp.int32),
             pltpu.SemaphoreType.DMA((7,)),
         ],
@@ -292,17 +349,19 @@
     parts = 2
     w1 = w_first.transpose(1, 2, 3, 4, 0).reshape(9, 3, C)
     w2, w3 = (w.transpose(2, 3, 4, 0, 1).reshape(27, C, C) for w in (w_second, w_third))
-    place, m1, m2, m3, bias = pl.pallas_call(
+    place, m1, m2, r2, m3, r3, bias = pl.pallas_call(
         functools.partial(prep_kernel, per, "gy"),
         out_shape=[
             jax.ShapeDtypeStruct((chunks, rows, wide), BF16),
             jax.ShapeDtypeStruct((2 * Z * C, 64), BF16),
-            jax.ShapeDtypeStruct((Z * C, 9 * Z * C), BF16),
-            jax.ShapeDtypeStruct((Z * C, 9 * Z * C), BF16),
+            jax.ShapeDtypeStruct((2, 6 * C, 8 * C), BF16),
+            jax.ShapeDtypeStruct((12 * C, 8 * C), BF16),
+            jax.ShapeDtypeStruct((2, 6 * C, 8 * C), BF16),
+            jax.ShapeDtypeStruct((12 * C, 8 * C), BF16),
             jax.ShapeDtypeStruct((3, Z * C, LANES), F32),
         ],
         in_specs=[vmem] * 9,
-        out_specs=[vmem] * 5,
+        out_specs=[vmem] * 7,
         scratch_shapes=[pltpu.VMEM((LANES, LANES), F32)],
         compiler_params=pltpu.CompilerParams(vmem_limit_bytes=24 * 1024 * 1024),
         cost_estimate=pl.CostEstimate(flops=200_000_000, bytes_accessed=3_000_000, transcendentals=0),
@@ -312,19 +371,21 @@
     return pl.pallas_call(
         functools.partial(conv_kernel, "gy", bricks),
         out_shape=jax.ShapeDtypeStruct((C, Z, YB, X), BF16),
-        in_specs=[vmem] * 6,
+        in_specs=[vmem] * 8,
         out_specs=pl.BlockSpec(memory_space=pl.ANY),
         scratch_shapes=[
-            pltpu.VMEM((3 * (YB + 4) * Z * C, X), BF16),
-            pltpu.VMEM((3 * (YB + 2) * Z * C, X), BF16),
-            pltpu.VMEM((parts, Z * C, YB, X // parts), F32),
-            pltpu.VMEM((parts, C, Z, YB, X // parts), BF16),
-            pltpu.SemaphoreType.DMA((parts,)),
+            pltpu.VMEM((2, (YB + 4) * 8 * C, X), BF16),
+            pltpu.VMEM(((YB + 4) * 2 * C, X), BF16),
+            pltpu.VMEM((2, (YB + 2) * 8 * C, X), BF16),
+            pltpu.VMEM(((YB + 2) * 2 * C, X), BF16),
+            pltpu.VMEM((parts, X // parts // LANES, Z * C * YB, LANES), F32),
+            pltpu.VMEM((parts, Z, C, YB, X // parts), BF16),
+            pltpu.SemaphoreType.DMA((parts, Z)),
         ],
         compiler_params=pltpu.CompilerParams(vmem_limit_bytes=40 * 1024 * 1024),
         cost_estimate=pl.CostEstimate(flops=4_000_000_000, bytes_accessed=6_000_000, transcendentals=0),
         name="convs",
-    )(arrived, place, m1, m2, m3, bias)
+    )(arrived, place, m1, m2, r2, m3, r3, bias)
 
 
 def solution(mesh):

time: 26 us -> 24.5 us (0.942)
  Pallas kernels: 9.95 us -> 8.04 us
  waiting for transfers between devices: 7.41 us -> 7.83 us
    pallas_call x1, Pallas kernels: 5.73 us -> 4.92 us  [on_device(): pl.pallas_call(functools.partial(conv_kernel, 'gy', bricks), out_shape=ja...]
    pallas_call x1, Pallas kernels: 2.85 us -> 2.16 us  [on_device(): pl.pallas_call(functools.partial(send_kernel, per, 'gy'), out_shape=jax.S...]
    all_to_all x1, waiting for transfers between devices: 7.41 us -> 7.83 us  [on_device(): lax.all_to_all(send.reshape(bricks, sent, sw), 'gy', split_axis=0, concat...]
    pallas_call x1, Pallas kernels: 1.37 us -> 0.96 us  [on_device(): pl.pallas_call(functools.partial(prep_kernel, per, 'gy'), out_shape=[jax....]
  transfers between devices with their start and end apart: 1 -> 1, of which waited for: 1 -> 1; matrix products, arithmetic and copies ran while one was open for 0% -> 0% of each run, Pallas kernels for 5% -> 4%
where the time goes in v3:
time: 24.5 us; the launch traced here: 24.2 us
  Pallas kernels  8.04 us (33%)
  waiting for transfers between devices  7.83 us (32%)
  starting transfers between devices  7.53 us (31%)
  local copies, waits for them, and re-layouts  0.68 us (3%)
    all_to_all x1, waiting for transfers between devices, on_device(): lax.all_to_all(send.reshape(bricks, sent, sw), 'gy', split_axis=0, concat...  7.83 us
    all_to_all x1, starting transfers between devices, on_device(): lax.all_to_all(send.reshape(bricks, sent, sw), 'gy', split_axis=0, concat...  7.53 us
    pallas_call x1, Pallas kernels, on_device(): pl.pallas_call(functools.partial(conv_kernel, 'gy', bricks), out_shape=ja...  4.92 us
    pallas_call x1, Pallas kernels, on_device(): pl.pallas_call(functools.partial(send_kernel, per, 'gy'), out_shape=jax.S...  2.16 us
    pallas_call x1, Pallas kernels, on_device(): pl.pallas_call(functools.partial(prep_kernel, per, 'gy'), out_shape=[jax....  0.96 us
    unnamed x18, local copies, waits for them, and re-layouts  0.68 us
  transfers between devices with their start and end apart: 1, of which 1 were waited for; matrix products, arithmetic and copies ran while one was open for 0% of the time, Pallas kernels for 4%

profile of v3, /device:TPU:0, one launch (start us, length us, event | category | flops | bytes accessed | tf_op | source)
XLA Modules:
  0.0 24.2 jit_solution(8546891448326930684)
XLA Ops:
  0.0 2.2 %send.1 = bf16[896,128]{1,0:T(8,128)(2,1)} custom-call(s32[1,512]{1,0:T(1,128)} %bitcast.24, s32[1,512]{1,0:T(1,128)} %bitcast.38, s32[1,512]{1,0:T(1,128)} %bitcast.39, s32[1,512]{1,0:T(1,128)} %bitcast.40, bf16[512,128]{1,0:T(8,128)(2,1)} %bitcast.36, bf16[64,16]{1,0:T(8,128)(2,1)} %bitcast.37, bf16[1024,128]{1,0:T(8,128)(2,1)} %bitcast.35), custom_call_target="tpu_custom_call" | custom-call | tf_op jit(solution)/shard_map/send/pallas_call | solution.py:324
  2.2 0.0 copy-start.1
  2.2 0.0 copy-start.2
  2.2 0.0 copy-start.6
  2.2 0.0 copy-start.7
  2.2 0.0 copy-start.8
  2.2 7.5 %all-to-all-start = ((bf16[16,56,128]{2,1,0:T(8,128)(2,1)}), bf16[16,56,128]{2,1,0:T(8,128)(2,1)S(1)}, u32[]{:S(2)}, u32[]{:S(2)}) async-start(bf16[16,56,128]{2,1,0:T(8,128)(2,1)} %bitcast.34), calls=%async_computation | async-start | bytes 458752 | tf_op jit(solution)/shard_map/all_to_all | solution.py:343
  9.8 0.0 copy-start.3
  9.8 0.0 copy-start.4
  9.8 0.0 copy-start.5
  9.8 0.0 copy-start
  9.8 0.0 copy-done.1
  9.8 0.0 copy-done.2
  9.8 0.0 copy-done.6
  9.9 0.0 copy-done.7
  9.9 0.0 copy-done.8
  9.9 0.6 %copy-done.3 = bf16[32,1,3,3,3]{0,4,3,2,1:T(4,128)(2,1)S(1)} copy-done((bf16[32,1,3,3,3]{0,4,3,2,1:T(4,128)(2,1)S(1)}, bf16[32,1,3,3,3]{0,4,3,2,1:T(4,128)(2,1)}, u32[]{:S(2)}) %copy-start.3) | copy-done | bytes 1752
  10.5 0.0 copy-done.4
  10.5 0.0 copy-done.5
  10.5 0.0 copy-done
  10.5 1.0 %prep.1 = (bf16[4,256,224]{2,1,0:T(8,128)(2,1)S(1)}, bf16[256,64]{1,0:T(8,128)(2,1)S(1)}, bf16[2,192,256]{2,1,0:T(8,128)(2,1)S(1)}, bf16[384,256]{1,0:T(8,128)(2...) custom-call(s32[1,512]{1,0:T(1,128)S(1)} %bitcast.25, ...), custom_call_target="tpu_custom_call" | custom-call | flops 200000000 | bytes 3000000 | tf_op jit(solution)/shard_map/prep/pallas_call | solution.py:352
  11.5 7.8 %all-to-all-done = bf16[16,56,128]{2,1,0:T(8,128)(2,1)S(1)} async-done(((bf16[16,56,128]{2,1,0:T(8,128)(2,1)}), bf16[16,56,128]{2,1,0:T(8,128)(2,1)S(1)}, u32[]{:S(2)}, u32[]{:S(2)}) %all-to-all-start) | async-done | bytes 229408 | tf_op jit(solution)/shard_map/all_to_all | solution.py:343
  19.3 4.9 %convs.1 = bf16[32,4,8,512]{3,2,1,0:T(8,128)(2,1)} custom-call(bf16[896,128]{1,0:T(8,128)(2,1)S(1)} %bitcast.23, bf16[4,256,224]{2,1,0:T(8,128)(2,1)S(1)} %get-tuple-element.12.place_ref, bf16[256,64]{1,0:T(8,128)(2,1)S(1)} %get-tuple-element.13.m1_ref, bf16[2,192,256]{2,1,0:T(8,128)(2,1)S(1)} %get-tuple-element.14.m2_ref, ...), custom_call_target="tpu_custom_call" | custom-call | flops 4000000000 | bytes 6000000 | tf_op jit(solution)/shard_map/convs/pallas_call | solution.py:371
Async XLA Ops:
  2.2 7.6 %copy-start.1 = (bf16[32,32,3,3,3]{1,0,4,3,2:T(8,128)(2,1)S(1)}, bf16[32,32,3,3,3]{1,0,4,3,2:T(8,128)(2,1)}, u32[]{:S(2)}) copy-start(bf16[32,32,3,3,3]{1,0,4,3,2:T(8,128)(2,1)} %param.26) | copy-start | bytes 165892
  2.2 7.6 %copy-start.2 = (bf16[32,32,3,3,3]{1,0,4,3,2:T(8,128)(2,1)S(1)}, bf16[32,32,3,3,3]{1,0,4,3,2:T(8,128)(2,1)}, u32[]{:S(2)}) copy-start(bf16[32,32,3,3,3]{1,0,4,3,2:T(8,128)(2,1)} %param.28) | copy-start | bytes 165892
  2.2 7.6 %copy-start.6 = (f32[32]{0:T(128)S(1)}, f32[32]{0:T(128)}, u32[]{:S(2)}) copy-start(f32[32]{0:T(128)} %param.25) | copy-start | bytes 388
  2.2 7.6 %copy-start.7 = (f32[32]{0:T(128)S(1)}, f32[32]{0:T(128)}, u32[]{:S(2)}) copy-start(f32[32]{0:T(128)} %param.27) | copy-start | bytes 388
  2.2 7.6 %copy-start.8 = (f32[32]{0:T(128)S(1)}, f32[32]{0:T(128)}, u32[]{:S(2)}) copy-start(f32[32]{0:T(128)} %param.29) | copy-start | bytes 388
  2.2 17.1 %all-to-all-start = ((bf16[16,56,128]{2,1,0:T(8,128)(2,1)}), bf16[16,56,128]{2,1,0:T(8,128)(2,1)S(1)}, u32[]{:S(2)}, u32[]{:S(2)}) async-start(bf16[16,56,128]{2,1,0:T(8,128)(2,1)} %bitcast.34), calls=%async_computation | async-start | bytes 458752 | tf_op jit(solution)/shard_map/all_to_all | solution.py:343
  9.8 0.7 %copy-start.3 = (bf16[32,1,3,3,3]{0,4,3,2,1:T(4,128)(2,1)S(1)}, bf16[32,1,3,3,3]{0,4,3,2,1:T(4,128)(2,1)}, u32[]{:S(2)}) copy-start(bf16[32,1,3,3,3]{0,4,3,2,1:T(4,128)(2,1)} %param.24) | copy-start | bytes 5188
  9.8 0.7 %copy-start.4 = (s32[512]{0:T(512)S(1)}, s32[512]{0:T(512)}, u32[]{:S(2)}) copy-start(s32[512]{0:T(512)} %param.18) | copy-start | bytes 6148
  9.8 0.7 %copy-start.5 = (s32[512]{0:T(512)S(1)}, s32[512]{0:T(512)}, u32[]{:S(2)}) copy-start(s32[512]{0:T(512)} %param.19) | copy-start | bytes 6148
  9.8 0.7 %copy-start = (s32[512,1]{0,1:T(1,128)S(1)}, s32[512,1]{0,1:T(1,128)}, u32[]{:S(2)}) copy-start(s32[512,1]{0,1:T(1,128)} %param.16) | copy-start | bytes 6148

commit v4 on v3

--- a/solution.py
+++ b/solution.py
@@ -14,7 +14,7 @@
 C = 32
 HALO = 3
 YW = YB + 2 * HALO
-CELLS = 16 * Z
+CELLS = YW * Z
 LANES = 128
 F32 = jnp.float32
 BF16 = jnp.bfloat16
@@ -277,7 +277,7 @@
         value = jnp.maximum(total + bias_of(2, cols), 0.0)
         for k in range(cols // LANES):
             staged[h, k, pl.ds(y, wide_m, stride=YB), :] = value[:, k * LANES : (k + 1) * LANES]
-        if h > 0 and y == YB // 2 - 1:
+        if h > 0 and y == YB - 2:
             flush(h - 1)
 
     def pack(h, z):

time: 24.5 us -> 24.4 us (level)
  no operation moved by 1% of the time
where the time goes in v4:
time: 24.4 us; the launch traced here: 24.1 us
  Pallas kernels  7.88 us (32%)
  waiting for transfers between devices  7.88 us (32%)
  starting transfers between devices  7.53 us (31%)
  local copies, waits for them, and re-layouts  0.68 us (3%)
    all_to_all x1, waiting for transfers between devices, on_device(): lax.all_to_all(send.reshape(bricks, sent, sw), 'gy', split_axis=0, concat...  7.88 us
    all_to_all x1, starting transfers between devices, on_device(): lax.all_to_all(send.reshape(bricks, sent, sw), 'gy', split_axis=0, concat...  7.53 us
    pallas_call x1, Pallas kernels, on_device(): pl.pallas_call(functools.partial(conv_kernel, 'gy', bricks), out_shape=ja...  4.82 us
    pallas_call x1, Pallas kernels, on_device(): pl.pallas_call(functools.partial(send_kernel, per, 'gy'), out_shape=jax.S...  2.16 us
    pallas_call x1, Pallas kernels, on_device(): pl.pallas_call(functools.partial(prep_kernel, per, 'gy'), out_shape=[jax....  0.9 us
    unnamed x18, local copies, waits for them, and re-layouts  0.68 us
  transfers between devices with their start and end apart: 1, of which 1 were waited for; matrix products, arithmetic and copies ran while one was open for 0% of the time, Pallas kernels for 4%

profile of v4, /device:TPU:0, one launch (start us, length us, event | category | flops | bytes accessed | tf_op | source)
XLA Modules:
  0.0 24.1 jit_solution(12024712416770845516)
XLA Ops:
  0.0 2.2 %send.1 = bf16[896,128]{1,0:T(8,128)(2,1)} custom-call(s32[1,512]{1,0:T(1,128)} %bitcast.24, s32[1,512]{1,0:T(1,128)} %bitcast.38, s32[1,512]{1,0:T(1,128)} %bitcast.39, s32[1,512]{1,0:T(1,128)} %bitcast.40, bf16[512,128]{1,0:T(8,128)(2,1)} %bitcast.36, bf16[64,16]{1,0:T(8,128)(2,1)} %bitcast.37, bf16[1024,128]{1,0:T(8,128)(2,1)} %bitcast.35), custom_call_target="tpu_custom_call" | custom-call | tf_op jit(solution)/shard_map/send/pallas_call | solution.py:324
  2.2 0.0 copy-start.1
  2.2 0.0 copy-start.2
  2.2 0.0 copy-start.6
  2.2 0.0 copy-start.7
  2.2 0.0 copy-start.8
  2.2 7.5 %all-to-all-start = ((bf16[16,56,128]{2,1,0:T(8,128)(2,1)}), bf16[16,56,128]{2,1,0:T(8,128)(2,1)S(1)}, u32[]{:S(2)}, u32[]{:S(2)}) async-start(bf16[16,56,128]{2,1,0:T(8,128)(2,1)} %bitcast.34), calls=%async_computation | async-start | bytes 458752 | tf_op jit(solution)/shard_map/all_to_all | solution.py:343
  9.8 0.0 copy-start.3
  9.8 0.0 copy-start.4
  9.8 0.0 copy-start.5
  9.8 0.0 copy-start
  9.8 0.0 copy-done.1
  9.8 0.0 copy-done.2
  9.8 0.0 copy-done.6
  9.9 0.0 copy-done.7
  9.9 0.0 copy-done.8
  9.9 0.6 %copy-done.3 = bf16[32,1,3,3,3]{0,4,3,2,1:T(4,128)(2,1)S(1)} copy-done((bf16[32,1,3,3,3]{0,4,3,2,1:T(4,128)(2,1)S(1)}, bf16[32,1,3,3,3]{0,4,3,2,1:T(4,128)(2,1)}, u32[]{:S(2)}) %copy-start.3) | copy-done | bytes 1752
  10.5 0.0 copy-done.4
  10.5 0.0 copy-done.5
  10.5 0.0 copy-done
  10.5 0.9 %prep.1 = (bf16[4,224,224]{2,1,0:T(8,128)(2,1)S(1)}, bf16[256,64]{1,0:T(8,128)(2,1)S(1)}, bf16[2,192,256]{2,1,0:T(8,128)(2,1)S(1)}, bf16[384,256]{1,0:T(8,128)(2...) custom-call(s32[1,512]{1,0:T(1,128)S(1)} %bitcast.25, ...), custom_call_target="tpu_custom_call" | custom-call | flops 200000000 | bytes 3000000 | tf_op jit(solution)/shard_map/prep/pallas_call | solution.py:352
  11.4 7.9 %all-to-all-done = bf16[16,56,128]{2,1,0:T(8,128)(2,1)S(1)} async-done(((bf16[16,56,128]{2,1,0:T(8,128)(2,1)}), bf16[16,56,128]{2,1,0:T(8,128)(2,1)S(1)}, u32[]{:S(2)}, u32[]{:S(2)}) %all-to-all-start) | async-done | bytes 229408 | tf_op jit(solution)/shard_map/all_to_all | solution.py:343
  19.3 4.8 %convs.1 = bf16[32,4,8,512]{3,2,1,0:T(8,128)(2,1)} custom-call(bf16[896,128]{1,0:T(8,128)(2,1)S(1)} %bitcast.23, bf16[4,224,224]{2,1,0:T(8,128)(2,1)S(1)} %get-tuple-element.12.place_ref, bf16[256,64]{1,0:T(8,128)(2,1)S(1)} %get-tuple-element.13.m1_ref, bf16[2,192,256]{2,1,0:T(8,128)(2,1)S(1)} %get-tuple-element.14.m2_ref, ...), custom_call_target="tpu_custom_call" | custom-call | flops 4000000000 | bytes 6000000 | tf_op jit(solution)/shard_map/convs/pallas_call | solution.py:371
Async XLA Ops:
  2.2 7.7 %copy-start.1 = (bf16[32,32,3,3,3]{1,0,4,3,2:T(8,128)(2,1)S(1)}, bf16[32,32,3,3,3]{1,0,4,3,2:T(8,128)(2,1)}, u32[]{:S(2)}) copy-start(bf16[32,32,3,3,3]{1,0,4,3,2:T(8,128)(2,1)} %param.26) | copy-start | bytes 165892
  2.2 7.6 %copy-start.2 = (bf16[32,32,3,3,3]{1,0,4,3,2:T(8,128)(2,1)S(1)}, bf16[32,32,3,3,3]{1,0,4,3,2:T(8,128)(2,1)}, u32[]{:S(2)}) copy-start(bf16[32,32,3,3,3]{1,0,4,3,2:T(8,128)(2,1)} %param.28) | copy-start | bytes 165892
  2.2 7.6 %copy-start.6 = (f32[32]{0:T(128)S(1)}, f32[32]{0:T(128)}, u32[]{:S(2)}) copy-start(f32[32]{0:T(128)} %param.25) | copy-start | bytes 388
  2.2 7.6 %copy-start.7 = (f32[32]{0:T(128)S(1)}, f32[32]{0:T(128)}, u32[]{:S(2)}) copy-start(f32[32]{0:T(128)} %param.27) | copy-start | bytes 388
  2.2 7.6 %copy-start.8 = (f32[32]{0:T(128)S(1)}, f32[32]{0:T(128)}, u32[]{:S(2)}) copy-start(f32[32]{0:T(128)} %param.29) | copy-start | bytes 388
  2.2 17.1 %all-to-all-start = ((bf16[16,56,128]{2,1,0:T(8,128)(2,1)}), bf16[16,56,128]{2,1,0:T(8,128)(2,1)S(1)}, u32[]{:S(2)}, u32[]{:S(2)}) async-start(bf16[16,56,128]{2,1,0:T(8,128)(2,1)} %bitcast.34), calls=%async_computation | async-start | bytes 458752 | tf_op jit(solution)/shard_map/all_to_all | solution.py:343
  9.8 0.7 %copy-start.3 = (bf16[32,1,3,3,3]{0,4,3,2,1:T(4,128)(2,1)S(1)}, bf16[32,1,3,3,3]{0,4,3,2,1:T(4,128)(2,1)}, u32[]{:S(2)}) copy-start(bf16[32,1,3,3,3]{0,4,3,2,1:T(4,128)(2,1)} %param.24) | copy-start | bytes 5188
  9.8 0.7 %copy-start.4 = (s32[512]{0:T(512)S(1)}, s32[512]{0:T(512)}, u32[]{:S(2)}) copy-start(s32[512]{0:T(512)} %param.18) | copy-start | bytes 6148
  9.8 0.7 %copy-start.5 = (s32[512]{0:T(512)S(1)}, s32[512]{0:T(512)}, u32[]{:S(2)}) copy-start(s32[512]{0:T(512)} %param.19) | copy-start | bytes 6148
  9.8 0.7 %copy-start = (s32[512,1]{0,1:T(1,128)S(1)}, s32[512,1]{0,1:T(1,128)}, u32[]{:S(2)}) copy-start(s32[512,1]{0,1:T(1,128)} %param.16) | copy-start | bytes 6148

commit v5 on v4

--- a/solution.py
+++ b/solution.py
@@ -281,9 +281,9 @@
             flush(h - 1)
 
     def pack(h, z):
-        for k in range(cols // LANES):
-            turned = staged[h, k, z * C * YB : (z + 1) * C * YB].astype(BF16).reshape(C, YB, LANES)
-            packed[h, z, :, :, k * LANES : (k + 1) * LANES] = turned
+        rows_of = slice(z * C * YB, (z + 1) * C * YB)
+        turned = [staged[h, k, rows_of].reshape(C, YB, LANES) for k in range(cols // LANES)]
+        packed[h, z] = jnp.concatenate(turned, axis=2).astype(BF16)
 
     def send(h, z):
         there = out_ref.at[:, z, :, pl.ds(h * cols, cols)]

time: 24.4 us -> 24.4 us (level)
  no operation moved by 1% of the time
where the time goes in v5:
time: 24.4 us; the launch traced here: 24.1 us
  Pallas kernels  7.88 us (32%)
  waiting for transfers between devices  7.88 us (32%)
  starting transfers between devices  7.53 us (31%)
  local copies, waits for them, and re-layouts  0.68 us (3%)
    all_to_all x1, waiting for transfers between devices, on_device(): lax.all_to_all(send.reshape(bricks, sent, sw), 'gy', split_axis=0, concat...  7.88 us
    all_to_all x1, starting transfers between devices, on_device(): lax.all_to_all(send.reshape(bricks, sent, sw), 'gy', split_axis=0, concat...  7.53 us
    pallas_call x1, Pallas kernels, on_device(): pl.pallas_call(functools.partial(conv_kernel, 'gy', bricks), out_shape=ja...  4.82 us
    pallas_call x1, Pallas kernels, on_device(): pl.pallas_call(functools.partial(send_kernel, per, 'gy'), out_shape=jax.S...  2.16 us
    pallas_call x1, Pallas kernels, on_device(): pl.pallas_call(functools.partial(prep_kernel, per, 'gy'), out_shape=[jax....  0.9 us
    unnamed x18, local copies, waits for them, and re-layouts  0.68 us
  transfers between devices with their start and end apart: 1, of which 1 were waited for; matrix products, arithmetic and copies ran while one was open for 0% of the time, Pallas kernels for 4%

profile of v5, /device:TPU:0, one launch (start us, length us, event | category | flops | bytes accessed | tf_op | source)
XLA Modules:
  0.0 24.1 jit_solution(11953275435253410798)
XLA Ops:
  0.0 2.2 %send.1 = bf16[896,128]{1,0:T(8,128)(2,1)} custom-call(s32[1,512]{1,0:T(1,128)} %bitcast.24, s32[1,512]{1,0:T(1,128)} %bitcast.38, s32[1,512]{1,0:T(1,128)} %bitcast.39, s32[1,512]{1,0:T(1,128)} %bitcast.40, bf16[512,128]{1,0:T(8,128)(2,1)} %bitcast.36, bf16[64,16]{1,0:T(8,128)(2,1)} %bitcast.37, bf16[1024,128]{1,0:T(8,128)(2,1)} %bitcast.35), custom_call_target="tpu_custom_call" | custom-call | tf_op jit(solution)/shard_map/send/pallas_call | solution.py:324
  2.2 0.0 copy-start.1
  2.2 0.0 copy-start.2
  2.2 0.0 copy-start.6
  2.2 0.0 copy-start.7
  2.2 0.0 copy-start.8
  2.2 7.5 %all-to-all-start = ((bf16[16,56,128]{2,1,0:T(8,128)(2,1)}), bf16[16,56,128]{2,1,0:T(8,128)(2,1)S(1)}, u32[]{:S(2)}, u32[]{:S(2)}) async-start(bf16[16,56,128]{2,1,0:T(8,128)(2,1)} %bitcast.34), calls=%async_computation | async-start | bytes 458752 | tf_op jit(solution)/shard_map/all_to_all | solution.py:343
  9.8 0.0 copy-start.3
  9.8 0.0 copy-start.4
  9.8 0.0 copy-start.5
  9.8 0.0 copy-start
  9.8 0.0 copy-done.1
  9.8 0.0 copy-done.2
  9.8 0.0 copy-done.6
  9.8 0.0 copy-done.7
  9.9 0.0 copy-done.8
  9.9 0.6 %copy-done.3 = bf16[32,1,3,3,3]{0,4,3,2,1:T(4,128)(2,1)S(1)} copy-done((bf16[32,1,3,3,3]{0,4,3,2,1:T(4,128)(2,1)S(1)}, bf16[32,1,3,3,3]{0,4,3,2,1:T(4,128)(2,1)}, u32[]{:S(2)}) %copy-start.3) | copy-done | bytes 1752
  10.5 0.0 copy-done.4
  10.5 0.0 copy-done.5
  10.5 0.0 copy-done
  10.5 0.9 %prep.1 = (bf16[4,224,224]{2,1,0:T(8,128)(2,1)S(1)}, bf16[256,64]{1,0:T(8,128)(2,1)S(1)}, bf16[2,192,256]{2,1,0:T(8,128)(2,1)S(1)}, bf16[384,256]{1,0:T(8,128)(2...) custom-call(s32[1,512]{1,0:T(1,128)S(1)} %bitcast.25, ...), custom_call_target="tpu_custom_call" | custom-call | flops 200000000 | bytes 3000000 | tf_op jit(solution)/shard_map/prep/pallas_call | solution.py:352
  11.4 7.9 %all-to-all-done = bf16[16,56,128]{2,1,0:T(8,128)(2,1)S(1)} async-done(((bf16[16,56,128]{2,1,0:T(8,128)(2,1)}), bf16[16,56,128]{2,1,0:T(8,128)(2,1)S(1)}, u32[]{:S(2)}, u32[]{:S(2)}) %all-to-all-start) | async-done | bytes 229408 | tf_op jit(solution)/shard_map/all_to_all | solution.py:343
  19.3 4.8 %convs.1 = bf16[32,4,8,512]{3,2,1,0:T(8,128)(2,1)} custom-call(bf16[896,128]{1,0:T(8,128)(2,1)S(1)} %bitcast.23, bf16[4,224,224]{2,1,0:T(8,128)(2,1)S(1)} %get-tuple-element.12.place_ref, bf16[256,64]{1,0:T(8,128)(2,1)S(1)} %get-tuple-element.13.m1_ref, bf16[2,192,256]{2,1,0:T(8,128)(2,1)S(1)} %get-tuple-element.14.m2_ref, ...), custom_call_target="tpu_custom_call" | custom-call | flops 4000000000 | bytes 6000000 | tf_op jit(solution)/shard_map/convs/pallas_call | solution.py:371
Async XLA Ops:
  2.2 7.6 %copy-start.1 = (bf16[32,32,3,3,3]{1,0,4,3,2:T(8,128)(2,1)S(1)}, bf16[32,32,3,3,3]{1,0,4,3,2:T(8,128)(2,1)}, u32[]{:S(2)}) copy-start(bf16[32,32,3,3,3]{1,0,4,3,2:T(8,128)(2,1)} %param.26) | copy-start | bytes 165892
  2.2 7.6 %copy-start.2 = (bf16[32,32,3,3,3]{1,0,4,3,2:T(8,128)(2,1)S(1)}, bf16[32,32,3,3,3]{1,0,4,3,2:T(8,128)(2,1)}, u32[]{:S(2)}) copy-start(bf16[32,32,3,3,3]{1,0,4,3,2:T(8,128)(2,1)} %param.28) | copy-start | bytes 165892
  2.2 7.6 %copy-start.6 = (f32[32]{0:T(128)S(1)}, f32[32]{0:T(128)}, u32[]{:S(2)}) copy-start(f32[32]{0:T(128)} %param.25) | copy-start | bytes 388
  2.2 7.6 %copy-start.7 = (f32[32]{0:T(128)S(1)}, f32[32]{0:T(128)}, u32[]{:S(2)}) copy-start(f32[32]{0:T(128)} %param.27) | copy-start | bytes 388
  2.2 7.6 %copy-start.8 = (f32[32]{0:T(128)S(1)}, f32[32]{0:T(128)}, u32[]{:S(2)}) copy-start(f32[32]{0:T(128)} %param.29) | copy-start | bytes 388
  2.2 17.1 %all-to-all-start = ((bf16[16,56,128]{2,1,0:T(8,128)(2,1)}), bf16[16,56,128]{2,1,0:T(8,128)(2,1)S(1)}, u32[]{:S(2)}, u32[]{:S(2)}) async-start(bf16[16,56,128]{2,1,0:T(8,128)(2,1)} %bitcast.34), calls=%async_computation | async-start | bytes 458752 | tf_op jit(solution)/shard_map/all_to_all | solution.py:343
  9.8 0.7 %copy-start.3 = (bf16[32,1,3,3,3]{0,4,3,2,1:T(4,128)(2,1)S(1)}, bf16[32,1,3,3,3]{0,4,3,2,1:T(4,128)(2,1)}, u32[]{:S(2)}) copy-start(bf16[32,1,3,3,3]{0,4,3,2,1:T(4,128)(2,1)} %param.24) | copy-start | bytes 5188
  9.8 0.7 %copy-start.4 = (s32[512]{0:T(512)S(1)}, s32[512]{0:T(512)}, u32[]{:S(2)}) copy-start(s32[512]{0:T(512)} %param.18) | copy-start | bytes 6148
  9.8 0.7 %copy-start.5 = (s32[512]{0:T(512)S(1)}, s32[512]{0:T(512)}, u32[]{:S(2)}) copy-start(s32[512]{0:T(512)} %param.19) | copy-start | bytes 6148
  9.8 0.7 %copy-start = (s32[512,1]{0,1:T(1,128)S(1)}, s32[512,1]{0,1:T(1,128)}, u32[]{:S(2)}) copy-start(s32[512,1]{0,1:T(1,128)} %param.16) | copy-start | bytes 6148

commit v6 on v5

--- a/solution.py
+++ b/solution.py
@@ -378,7 +378,7 @@
             pltpu.VMEM(((YB + 4) * 2 * C, X), BF16),
             pltpu.VMEM((2, (YB + 2) * 8 * C, X), BF16),
             pltpu.VMEM(((YB + 2) * 2 * C, X), BF16),
-            pltpu.VMEM((parts, X // parts // LANES, Z * C * YB, LANES), F32),
+            pltpu.VMEM((parts, X // parts // LANES, (Z * C + 1) * YB, LANES), F32),
             pltpu.VMEM((parts, Z, C, YB, X // parts), BF16),
             pltpu.SemaphoreType.DMA((parts, Z)),
         ],

time: 24.4 us -> 24.4 us (level)
  no operation moved by 1% of the time
where the time goes in v6:
time: 24.4 us; the launch traced here: 24.1 us
  Pallas kernels  7.89 us (32%)
  waiting for transfers between devices  7.88 us (32%)
  starting transfers between devices  7.53 us (31%)
  local copies, waits for them, and re-layouts  0.68 us (3%)
    all_to_all x1, waiting for transfers between devices, on_device(): lax.all_to_all(send.reshape(bricks, sent, sw), 'gy', split_axis=0, concat...  7.88 us
    all_to_all x1, starting transfers between devices, on_device(): lax.all_to_all(send.reshape(bricks, sent, sw), 'gy', split_axis=0, concat...  7.53 us
    pallas_call x1, Pallas kernels, on_device(): pl.pallas_call(functools.partial(conv_kernel, 'gy', bricks), out_shape=ja...  4.83 us
    pallas_call x1, Pallas kernels, on_device(): pl.pallas_call(functools.partial(send_kernel, per, 'gy'), out_shape=jax.S...  2.17 us
    pallas_call x1, Pallas kernels, on_device(): pl.pallas_call(functools.partial(prep_kernel, per, 'gy'), out_shape=[jax....  0.9 us
    unnamed x18, local copies, waits for them, and re-layouts  0.68 us
  transfers between devices with their start and end apart: 1, of which 1 were waited for; matrix products, arithmetic and copies ran while one was open for 0% of the time, Pallas kernels for 4%

profile of v6, /device:TPU:0, one launch (start us, length us, event | category | flops | bytes accessed | tf_op | source)
XLA Modules:
  0.0 24.1 jit_solution(4740921789414767433)
XLA Ops:
  0.0 2.2 %send.1 = bf16[896,128]{1,0:T(8,128)(2,1)} custom-call(s32[1,512]{1,0:T(1,128)} %bitcast.24, s32[1,512]{1,0:T(1,128)} %bitcast.38, s32[1,512]{1,0:T(1,128)} %bitcast.39, s32[1,512]{1,0:T(1,128)} %bitcast.40, bf16[512,128]{1,0:T(8,128)(2,1)} %bitcast.36, bf16[64,16]{1,0:T(8,128)(2,1)} %bitcast.37, bf16[1024,128]{1,0:T(8,128)(2,1)} %bitcast.35), custom_call_target="tpu_custom_call" | custom-call | tf_op jit(solution)/shard_map/send/pallas_call | solution.py:324
  2.2 0.0 copy-start.1
  2.2 0.0 copy-start.2
  2.2 0.0 copy-start.6
  2.2 0.0 copy-start.7
  2.2 0.0 copy-start.8
  2.2 7.5 %all-to-all-start = ((bf16[16,56,128]{2,1,0:T(8,128)(2,1)}), bf16[16,56,128]{2,1,0:T(8,128)(2,1)S(1)}, u32[]{:S(2)}, u32[]{:S(2)}) async-start(bf16[16,56,128]{2,1,0:T(8,128)(2,1)} %bitcast.34), calls=%async_computation | async-start | bytes 458752 | tf_op jit(solution)/shard_map/all_to_all | solution.py:343
  9.8 0.0 copy-start.3
  9.8 0.0 copy-start.4
  9.8 0.0 copy-start.5
  9.8 0.0 copy-start
  9.8 0.0 copy-done.1
  9.8 0.0 copy-done.2
  9.8 0.0 copy-done.6
  9.9 0.0 copy-done.7
  9.9 0.0 copy-done.8
  9.9 0.6 %copy-done.3 = bf16[32,1,3,3,3]{0,4,3,2,1:T(4,128)(2,1)S(1)} copy-done((bf16[32,1,3,3,3]{0,4,3,2,1:T(4,128)(2,1)S(1)}, bf16[32,1,3,3,3]{0,4,3,2,1:T(4,128)(2,1)}, u32[]{:S(2)}) %copy-start.3) | copy-done | bytes 1752
  10.5 0.0 copy-done.4
  10.5 0.0 copy-done.5
  10.5 0.0 copy-done
  10.5 0.9 %prep.1 = (bf16[4,224,224]{2,1,0:T(8,128)(2,1)S(1)}, bf16[256,64]{1,0:T(8,128)(2,1)S(1)}, bf16[2,192,256]{2,1,0:T(8,128)(2,1)S(1)}, bf16[384,256]{1,0:T(8,128)(2...) custom-call(s32[1,512]{1,0:T(1,128)S(1)} %bitcast.25, ...), custom_call_target="tpu_custom_call" | custom-call | flops 200000000 | bytes 3000000 | tf_op jit(solution)/shard_map/prep/pallas_call | solution.py:352
  11.4 7.9 %all-to-all-done = bf16[16,56,128]{2,1,0:T(8,128)(2,1)S(1)} async-done(((bf16[16,56,128]{2,1,0:T(8,128)(2,1)}), bf16[16,56,128]{2,1,0:T(8,128)(2,1)S(1)}, u32[]{:S(2)}, u32[]{:S(2)}) %all-to-all-start) | async-done | bytes 229408 | tf_op jit(solution)/shard_map/all_to_all | solution.py:343
  19.3 4.8 %convs.1 = bf16[32,4,8,512]{3,2,1,0:T(8,128)(2,1)} custom-call(bf16[896,128]{1,0:T(8,128)(2,1)S(1)} %bitcast.23, bf16[4,224,224]{2,1,0:T(8,128)(2,1)S(1)} %get-tuple-element.12.place_ref, bf16[256,64]{1,0:T(8,128)(2,1)S(1)} %get-tuple-element.13.m1_ref, bf16[2,192,256]{2,1,0:T(8,128)(2,1)S(1)} %get-tuple-element.14.m2_ref, ...), custom_call_target="tpu_custom_call" | custom-call | flops 4000000000 | bytes 6000000 | tf_op jit(solution)/shard_map/convs/pallas_call | solution.py:371
Async XLA Ops:
  2.2 7.6 %copy-start.1 = (bf16[32,32,3,3,3]{1,0,4,3,2:T(8,128)(2,1)S(1)}, bf16[32,32,3,3,3]{1,0,4,3,2:T(8,128)(2,1)}, u32[]{:S(2)}) copy-start(bf16[32,32,3,3,3]{1,0,4,3,2:T(8,128)(2,1)} %param.26) | copy-start | bytes 165892
  2.2 7.6 %copy-start.2 = (bf16[32,32,3,3,3]{1,0,4,3,2:T(8,128)(2,1)S(1)}, bf16[32,32,3,3,3]{1,0,4,3,2:T(8,128)(2,1)}, u32[]{:S(2)}) copy-start(bf16[32,32,3,3,3]{1,0,4,3,2:T(8,128)(2,1)} %param.28) | copy-start | bytes 165892
  2.2 7.6 %copy-start.6 = (f32[32]{0:T(128)S(1)}, f32[32]{0:T(128)}, u32[]{:S(2)}) copy-start(f32[32]{0:T(128)} %param.25) | copy-start | bytes 388
  2.2 7.6 %copy-start.7 = (f32[32]{0:T(128)S(1)}, f32[32]{0:T(128)}, u32[]{:S(2)}) copy-start(f32[32]{0:T(128)} %param.27) | copy-start | bytes 388
  2.2 7.6 %copy-start.8 = (f32[32]{0:T(128)S(1)}, f32[32]{0:T(128)}, u32[]{:S(2)}) copy-start(f32[32]{0:T(128)} %param.29) | copy-start | bytes 388
  2.2 17.1 %all-to-all-start = ((bf16[16,56,128]{2,1,0:T(8,128)(2,1)}), bf16[16,56,128]{2,1,0:T(8,128)(2,1)S(1)}, u32[]{:S(2)}, u32[]{:S(2)}) async-start(bf16[16,56,128]{2,1,0:T(8,128)(2,1)} %bitcast.34), calls=%async_computation | async-start | bytes 458752 | tf_op jit(solution)/shard_map/all_to_all | solution.py:343
  9.8 0.7 %copy-start.3 = (bf16[32,1,3,3,3]{0,4,3,2,1:T(4,128)(2,1)S(1)}, bf16[32,1,3,3,3]{0,4,3,2,1:T(4,128)(2,1)}, u32[]{:S(2)}) copy-start(bf16[32,1,3,3,3]{0,4,3,2,1:T(4,128)(2,1)} %param.24) | copy-start | bytes 5188
  9.8 0.7 %copy-start.4 = (s32[512]{0:T(512)S(1)}, s32[512]{0:T(512)}, u32[]{:S(2)}) copy-start(s32[512]{0:T(512)} %param.18) | copy-start | bytes 6148
  9.8 0.7 %copy-start.5 = (s32[512]{0:T(512)S(1)}, s32[512]{0:T(512)}, u32[]{:S(2)}) copy-start(s32[512]{0:T(512)} %param.19) | copy-start | bytes 6148
  9.8 0.7 %copy-start = (s32[512,1]{0,1:T(1,128)S(1)}, s32[512,1]{0,1:T(1,128)}, u32[]{:S(2)}) copy-start(s32[512,1]{0,1:T(1,128)} %param.16) | copy-start | bytes 6148

commit v7 on v6

--- a/solution.py
+++ b/solution.py
@@ -277,7 +277,7 @@
         value = jnp.maximum(total + bias_of(2, cols), 0.0)
         for k in range(cols // LANES):
             staged[h, k, pl.ds(y, wide_m, stride=YB), :] = value[:, k * LANES : (k + 1) * LANES]
-        if h > 0 and y == YB - 2:
+        if h > 0 and y == YB - 1:
             flush(h - 1)
 
     def pack(h, z):

time: 24.4 us -> 24.5 us (level)
  no operation moved by 1% of the time
where the time goes in v7:
time: 24.5 us; the launch traced here: 24.1 us
  Pallas kernels  7.9 us (32%)
  waiting for transfers between devices  7.88 us (32%)
  starting transfers between devices  7.53 us (31%)
  local copies, waits for them, and re-layouts  0.68 us (3%)
    all_to_all x1, waiting for transfers between devices, on_device(): lax.all_to_all(send.reshape(bricks, sent, sw), 'gy', split_axis=0, concat...  7.88 us
    all_to_all x1, starting transfers between devices, on_device(): lax.all_to_all(send.reshape(bricks, sent, sw), 'gy', split_axis=0, concat...  7.53 us
    pallas_call x1, Pallas kernels, on_device(): pl.pallas_call(functools.partial(conv_kernel, 'gy', bricks), out_shape=ja...  4.83 us
    pallas_call x1, Pallas kernels, on_device(): pl.pallas_call(functools.partial(send_kernel, per, 'gy'), out_shape=jax.S...  2.17 us
    pallas_call x1, Pallas kernels, on_device(): pl.pallas_call(functools.partial(prep_kernel, per, 'gy'), out_shape=[jax....  0.9 us
    unnamed x18, local copies, waits for them, and re-layouts  0.68 us
  transfers between devices with their start and end apart: 1, of which 1 were waited for; matrix products, arithmetic and copies ran while one was open for 0% of the time, Pallas kernels for 4%

profile of v7, /device:TPU:0, one launch (start us, length us, event | category | flops | bytes accessed | tf_op | source)
XLA Modules:
  0.0 24.1 jit_solution(4740921789414767433)
XLA Ops:
  0.0 2.2 %send.1 = bf16[896,128]{1,0:T(8,128)(2,1)} custom-call(s32[1,512]{1,0:T(1,128)} %bitcast.24, s32[1,512]{1,0:T(1,128)} %bitcast.38, s32[1,512]{1,0:T(1,128)} %bitcast.39, s32[1,512]{1,0:T(1,128)} %bitcast.40, bf16[512,128]{1,0:T(8,128)(2,1)} %bitcast.36, bf16[64,16]{1,0:T(8,128)(2,1)} %bitcast.37, bf16[1024,128]{1,0:T(8,128)(2,1)} %bitcast.35), custom_call_target="tpu_custom_call" | custom-call | tf_op jit(solution)/shard_map/send/pallas_call | solution.py:324
  2.2 0.0 copy-start.1
  2.2 0.0 copy-start.2
  2.2 0.0 copy-start.6
  2.2 0.0 copy-start.7
  2.2 0.0 copy-start.8
  2.2 7.5 %all-to-all-start = ((bf16[16,56,128]{2,1,0:T(8,128)(2,1)}), bf16[16,56,128]{2,1,0:T(8,128)(2,1)S(1)}, u32[]{:S(2)}, u32[]{:S(2)}) async-start(bf16[16,56,128]{2,1,0:T(8,128)(2,1)} %bitcast.34), calls=%async_computation | async-start | bytes 458752 | tf_op jit(solution)/shard_map/all_to_all | solution.py:343
  9.8 0.0 copy-start.3
  9.8 0.0 copy-start.4
  9.8 0.0 copy-start.5
  9.8 0.0 copy-start
  9.8 0.0 copy-done.1
  9.8 0.0 copy-done.2
  9.8 0.0 copy-done.6
  9.8 0.0 copy-done.7
  9.9 0.0 copy-done.8
  9.9 0.6 %copy-done.3 = bf16[32,1,3,3,3]{0,4,3,2,1:T(4,128)(2,1)S(1)} copy-done((bf16[32,1,3,3,3]{0,4,3,2,1:T(4,128)(2,1)S(1)}, bf16[32,1,3,3,3]{0,4,3,2,1:T(4,128)(2,1)}, u32[]{:S(2)}) %copy-start.3) | copy-done | bytes 1752
  10.5 0.0 copy-done.4
  10.5 0.0 copy-done.5
  10.5 0.0 copy-done
  10.5 0.9 %prep.1 = (bf16[4,224,224]{2,1,0:T(8,128)(2,1)S(1)}, bf16[256,64]{1,0:T(8,128)(2,1)S(1)}, bf16[2,192,256]{2,1,0:T(8,128)(2,1)S(1)}, bf16[384,256]{1,0:T(8,128)(2...) custom-call(s32[1,512]{1,0:T(1,128)S(1)} %bitcast.25, ...), custom_call_target="tpu_custom_call" | custom-call | flops 200000000 | bytes 3000000 | tf_op jit(solution)/shard_map/prep/pallas_call | solution.py:352
  11.4 7.9 %all-to-all-done = bf16[16,56,128]{2,1,0:T(8,128)(2,1)S(1)} async-done(((bf16[16,56,128]{2,1,0:T(8,128)(2,1)}), bf16[16,56,128]{2,1,0:T(8,128)(2,1)S(1)}, u32[]{:S(2)}, u32[]{:S(2)}) %all-to-all-start) | async-done | bytes 229408 | tf_op jit(solution)/shard_map/all_to_all | solution.py:343
  19.3 4.8 %convs.1 = bf16[32,4,8,512]{3,2,1,0:T(8,128)(2,1)} custom-call(bf16[896,128]{1,0:T(8,128)(2,1)S(1)} %bitcast.23, bf16[4,224,224]{2,1,0:T(8,128)(2,1)S(1)} %get-tuple-element.12.place_ref, bf16[256,64]{1,0:T(8,128)(2,1)S(1)} %get-tuple-element.13.m1_ref, bf16[2,192,256]{2,1,0:T(8,128)(2,1)S(1)} %get-tuple-element.14.m2_ref, ...), custom_call_target="tpu_custom_call" | custom-call | flops 4000000000 | bytes 6000000 | tf_op jit(solution)/shard_map/convs/pallas_call | solution.py:371
Async XLA Ops:
  2.2 7.6 %copy-start.1 = (bf16[32,32,3,3,3]{1,0,4,3,2:T(8,128)(2,1)S(1)}, bf16[32,32,3,3,3]{1,0,4,3,2:T(8,128)(2,1)}, u32[]{:S(2)}) copy-start(bf16[32,32,3,3,3]{1,0,4,3,2:T(8,128)(2,1)} %param.26) | copy-start | bytes 165892
  2.2 7.6 %copy-start.2 = (bf16[32,32,3,3,3]{1,0,4,3,2:T(8,128)(2,1)S(1)}, bf16[32,32,3,3,3]{1,0,4,3,2:T(8,128)(2,1)}, u32[]{:S(2)}) copy-start(bf16[32,32,3,3,3]{1,0,4,3,2:T(8,128)(2,1)} %param.28) | copy-start | bytes 165892
  2.2 7.6 %copy-start.6 = (f32[32]{0:T(128)S(1)}, f32[32]{0:T(128)}, u32[]{:S(2)}) copy-start(f32[32]{0:T(128)} %param.25) | copy-start | bytes 388
  2.2 7.6 %copy-start.7 = (f32[32]{0:T(128)S(1)}, f32[32]{0:T(128)}, u32[]{:S(2)}) copy-start(f32[32]{0:T(128)} %param.27) | copy-start | bytes 388
  2.2 7.6 %copy-start.8 = (f32[32]{0:T(128)S(1)}, f32[32]{0:T(128)}, u32[]{:S(2)}) copy-start(f32[32]{0:T(128)} %param.29) | copy-start | bytes 388
  2.2 17.1 %all-to-all-start = ((bf16[16,56,128]{2,1,0:T(8,128)(2,1)}), bf16[16,56,128]{2,1,0:T(8,128)(2,1)S(1)}, u32[]{:S(2)}, u32[]{:S(2)}) async-start(bf16[16,56,128]{2,1,0:T(8,128)(2,1)} %bitcast.34), calls=%async_computation | async-start | bytes 458752 | tf_op jit(solution)/shard_map/all_to_all | solution.py:343
  9.8 0.7 %copy-start.3 = (bf16[32,1,3,3,3]{0,4,3,2,1:T(4,128)(2,1)S(1)}, bf16[32,1,3,3,3]{0,4,3,2,1:T(4,128)(2,1)}, u32[]{:S(2)}) copy-start(bf16[32,1,3,3,3]{0,4,3,2,1:T(4,128)(2,1)} %param.24) | copy-start | bytes 5188
  9.8 0.7 %copy-start.4 = (s32[512]{0:T(512)S(1)}, s32[512]{0:T(512)}, u32[]{:S(2)}) copy-start(s32[512]{0:T(512)} %param.18) | copy-start | bytes 6148
  9.8 0.7 %copy-start.5 = (s32[512]{0:T(512)S(1)}, s32[512]{0:T(512)}, u32[]{:S(2)}) copy-start(s32[512]{0:T(512)} %param.19) | copy-start | bytes 6148
  9.8 0.7 %copy-start = (s32[512,1]{0,1:T(1,128)S(1)}, s32[512,1]{0,1:T(1,128)}, u32[]{:S(2)}) copy-start(s32[512,1]{0,1:T(1,128)} %param.16) | copy-start | bytes 6148
